TPU v7x, 128 devices: a whole 4x4x4 slice. The times are simulated.
128 devices in a mesh: az: 8 (over x_hi, z), acq: 16 (over x_lo, y, core).
Axes of the slice: x: 4 (x_hi: 2, x_lo: 2; x = x_hi * 2 + x_lo), y: 4, z: 4, core: 2. Of those that a mesh axis runs over, the one named last changes fastest.
Arguments:
- radar_stack: bfloat16 [2, 64, 8192, 256], P(None, 'acq', 'az'), may hold values from -8 to 8
- band_taps: bfloat16 [2, 64, 127], P(None, 'acq'), may hold values from -0.375 to 0.375
- pair_list: int32 [256, 2], replicated, may hold values from 0 to 63, as said below
Outputs:
- acquisition_phase: float32 [64, 131072], P(None, ('az', 'acq'))
Inputs may be any that keep to these rules, and one draw needn't show every extreme that they name: `pair_list`: row p has reference p // 4. Cut the acquisitions into as many consecutive equal groups as the acq axis has devices, closed into a cycle: the 4 secondaries of one reference lie one in each of the 4 groups that follow the reference's group on the cycle, in an order drawn anew for every reference.
All inputs are finite; a program needn't handle non-finite values.
Results may differ from a plain program's by a relative error of at most 0.0046.
Values may be sent and summed in bfloat16 or wider, within the bound.
No kernel may reach another device: no remote copies, remote signals or barrier semaphores. Data moves between devices by JAX's collectives and lax.ppermute only.
A program may use at most 128 MiB of HBM per device.

v0:
```python
import jax
import jax.numpy as jnp
from jax import lax
from jax.sharding import PartitionSpec as P

LOOK = 4
REACH = 4


ridge_weight = 1.0


def extended(array, sides, width):
    for axis, dim in sides:
        size, length = (lax.axis_size(axis), array.shape[dim])
        up = [(i, (i + 1) % size) for i in range(size - 1)]
        down = [(j, i) for i, j in up]
        last = lax.slice_in_dim(array, length - width, length, axis=dim)
        first = lax.slice_in_dim(array, 0, width, axis=dim)
        before = lax.ppermute(last, axis, up)
        after = lax.ppermute(first, axis, down)
        array = jnp.concatenate([before, array, after], axis=dim)
    return array


def from_behind(value, axis, steps):
    count = lax.axis_size(axis)
    pairs = [(source, (source + steps) % count) for source in range(count)]
    return lax.ppermute(value, axis, pairs)


def band_matrix(taps, rows):
    width = rows + taps.shape[-1] - 1
    lead = taps.shape[:-1]
    line = jnp.concatenate([taps, jnp.zeros(lead + (rows,), taps.dtype)], axis=-1)
    tiled = jnp.tile(line, (1,) * len(lead) + (rows,))
    return tiled[..., : rows * width].reshape(lead + (rows, width))


def pool_matrix(columns):
    flat = jnp.arange(LOOK * columns, dtype=jnp.int32)[:, None]
    target = jnp.arange(columns // LOOK, dtype=jnp.int32)[None, :]
    return jnp.where(flat % columns // LOOK == target, 1.0 / (LOOK * LOOK), 0.0).astype(jnp.float32)


def linear_phase(first, second):
    first = first.astype(jnp.float32)
    second = second.astype(jnp.float32)
    real = first[0] * second[0] + first[1] * second[1]
    imag = first[1] * second[0] - first[0] * second[1]
    count, rows, columns = real.shape
    pooling = pool_matrix(columns)
    real = jnp.einsum(
        "cbk,kp->cbp",
        real.reshape(count, rows // LOOK, LOOK * columns),
        pooling,
        precision=lax.Precision.HIGHEST,
        preferred_element_type=jnp.float32,
    )
    imag = jnp.einsum(
        "cbk,kp->cbp",
        imag.reshape(count, rows // LOOK, LOOK * columns),
        pooling,
        precision=lax.Precision.HIGHEST,
        preferred_element_type=jnp.float32,
    )
    magnitude = jnp.sqrt(real * real + imag * imag)
    return (imag / jnp.maximum(magnitude, 1.0)).reshape(count, -1)


def per_device(radar_stack, band_taps, pair_list):
    groups = lax.axis_size("acq")
    group = lax.axis_index("acq")
    local_count = radar_stack.shape[1]
    rows = radar_stack.shape[2]
    half = (band_taps.shape[2] - 1) // 2
    padded = extended(radar_stack, (("az", 2),), half)
    matrix = band_matrix(band_taps, rows)

    def convolve(taps_part, image_part):
        return jnp.einsum("arl,alg->arg", taps_part, image_part, preferred_element_type=jnp.float32)

    real_part = convolve(matrix[0], padded[0]) - convolve(matrix[1], padded[1])
    imag_part = convolve(matrix[0], padded[1]) + convolve(matrix[1], padded[0])
    filtered = jnp.stack([real_part, imag_part]).astype(jnp.bfloat16)
    total_acq = local_count * groups
    labels = jnp.arange(total_acq, dtype=jnp.int32)
    incidence = (pair_list[:, 1:2] == labels).astype(jnp.float32) - (
        pair_list[:, 0:1] == labels
    ).astype(jnp.float32)
    normal = jnp.dot(
        incidence.T, incidence, precision=lax.Precision.HIGHEST, preferred_element_type=jnp.float32
    ) + ridge_weight * jnp.eye(total_acq, dtype=jnp.float32)
    lower = jnp.linalg.cholesky(normal)
    partial_solve = lax.linalg.triangular_solve(lower, incidence.T, left_side=True, lower=True)
    inverse_map = lax.linalg.triangular_solve(
        lower, partial_solve, left_side=True, lower=True, transpose_a=True
    )
    own_pairs = lax.dynamic_slice_in_dim(
        pair_list, group * (REACH * local_count), REACH * local_count, 0
    )
    secondary = own_pairs[:, 1].reshape(local_count, REACH)
    offset = (secondary // local_count - group) % groups
    slot = secondary % local_count
    looks = []
    current = filtered
    for step in range(1, REACH + 1):
        current = from_behind(current, "acq", -1)
        chosen = jnp.sum(jnp.where(offset == step, slot, 0), axis=1)
        partner = jnp.take(current, chosen, axis=1)
        looks.append(linear_phase(filtered, partner))
    phases = jnp.stack(looks)
    steps_row = jnp.arange(1, REACH + 1, dtype=jnp.int32)
    picker = (offset[:, :, None] == steps_row).astype(jnp.float32)
    pair_phase = jnp.einsum(
        "ajk,kap->ajp",
        picker,
        phases,
        precision=lax.Precision.HIGHEST,
        preferred_element_type=jnp.float32,
    ).reshape(REACH * local_count, -1)
    own_map = lax.dynamic_slice_in_dim(
        inverse_map, group * (REACH * local_count), REACH * local_count, 1
    )
    summed = lax.psum_scatter(
        lax.dot_general(
            pair_phase,
            own_map,
            (((0,), (1,)), ((), ())),
            precision=lax.Precision.HIGHEST,
            preferred_element_type=jnp.float32,
        ),
        "acq",
        scatter_dimension=0,
        tiled=True,
    )
    return summed.T


def solution(mesh):
    return jax.shard_map(
        per_device,
        mesh=mesh,
        in_specs=(P(None, "acq", "az", None), P(None, "acq", None), P()),
        out_specs=P(None, ("az", "acq")),
        check_vma=False,
    )
```

profile of v0, /device:TPU:4, one launch (start us, length us, event | category | flops | bytes accessed | tf_op | source)
XLA Modules:
  0.0 639.0 jit_solution(17971231113492351225)
XLA Ops:
  6.5 1.1 fusion.119
  7.6 3.8 collective-permute-start
  11.5 5.6 collective-permute-start.1
  17.1 0.7 concatenate.6
  17.8 6.8 %tile.4 = bf16[2,4,1024,1151]{3,2,1,0:T(8,128)(2,1)} broadcast(bf16[2,4,1151]{2,1,0:T(4,128)(2,1)S(1)} %concatenate.6), dimensions={0,1,3} | broadcast | bytes 18876400 | tf_op jit(solution)/shard_map/tile | solution.py:36
  24.6 54.5 %tile.10 = bf16[2,4,1178624]{2,1,0:T(4,128)(2,1)} reshape(bf16[2,4,1024,1151]{3,2,1,0:T(8,128)(2,1)} %tile.4) | data formatting | bytes 37715968 | tf_op jit(solution)/shard_map/tile | solution.py:36
  79.1 19.0 %fusion.118 = (bf16[1,4,1177600]{2,1,0:T(4,128)(2,1)}, bf16[1,4,1177600]{2,1,0:T(4,128)(2,1)}) fusion(bf16[2,4,1178624]{2,1,0:T(4,128)(2,1)} %tile.10), kind=kLoop, calls=%fused_computation.191 | loop fusion | bytes 37683200 | tf_op jit(solution)/shard_map/slice | solution.py:83
  98.0 24.0 %reshape.237 = bf16[4710400]{0:T(1024)(128)(2,1)} reshape(bf16[1,4,1177600]{2,1,0:T(4,128)(2,1)} %get-tuple-element.12) | data formatting | bytes 18841600
  122.1 20.7 %squeeze.10 = bf16[4,1024,1150]{2,1,0:T(8,128)(2,1)} reshape(bf16[4710400]{0:T(1024)(128)(2,1)} %reshape.237) | data formatting | bytes 18841600 | tf_op jit(solution)/shard_map/squeeze | solution.py:83
  142.7 23.8 %reshape.239 = bf16[4710400]{0:T(1024)(128)(2,1)} reshape(bf16[1,4,1177600]{2,1,0:T(4,128)(2,1)} %get-tuple-element.11) | data formatting | bytes 18841600
  166.6 20.6 %squeeze.8 = bf16[4,1024,1150]{2,1,0:T(8,128)(2,1)} reshape(bf16[4710400]{0:T(1024)(128)(2,1)} %reshape.239) | data formatting | bytes 18841600 | tf_op jit(solution)/shard_map/squeeze | solution.py:83
  187.2 25.7 %concatenate.7 = bf16[2,4,1150,256]{3,2,1,0:T(8,128)(2,1)} concatenate(bf16[2,4,63,256]{3,2,1,0:T(8,128)(2,1)S(1)} %collective-permute-done, bf16[2,4,1024,256]{3,2,1,0:T(8,128)(2,1)} %param.5, bf16[2,4,63,256]{3,2,1,0:T(8,128)(2,1)S(1)} %collective-permute-done.1), dimensions={2} | concatenate | bytes 9420800 | tf_op jit(solution)/shard_map/concatenate | solution.py:22
  212.9 9.4 %fusion.5 = f32[4,1024,256]{2,1,0:T(8,128)} fusion(bf16[4,1024,1150]{2,1,0:T(8,128)(2,1)} %squeeze.10, bf16[2,4,1150,256]{3,2,1,0:T(8,128)(2,1)} %concatenate.7), kind=kOutput, calls=%fused_computation.27 | convolution fusion | flops 2411724800 | bytes 15990784 | tf_op jit(solution)/shard_map/arl,alg->arg/dot_general | solution.py:81
  222.3 4.4 fusion.2
  226.7 8.6 %fusion = bf16[1,4,1024,256]{3,2,1,0:T(8,128)(2,1)S(1)} fusion(f32[4,1024,256]{2,1,0:T(8,128)} %fusion.5, bf16[4,1024,1150]{2,1,0:T(8,128)(2,1)} %squeeze.8, bf16[2,4,1150,256]{3,2,1,0:T(8,128)(2,1)} %concatenate.7), kind=kOutput, calls=%fused_computation.22 | convolution fusion | flops 2413821952 | bytes 18087936 | tf_op jit(solution)/shard_map/arl,alg->arg/dot_general | solution.py:81
  235.4 4.8 fusion.1
  240.3 0.4 pad_maximum_fusion
  240.7 0.9 copy-done.4
  241.6 2.5 collective-permute-start.2
  244.1 46.0 %collective-permute-done.2 = bf16[2,4,1024,256]{3,2,1,0:T(8,128)(2,1)S(1)} collective-permute-done((bf16[2,4,1024,256]{3,2,1,0:T(8,128)(2,1)S(1)}, bf16[2,4,1024,256]{3,2,1,0:T(8,128)(2,1)S(1)}, u32[]{:S(2)}, u32[]{:S(2)}) %collective-permute-start.2) | collective-permute-done | bytes 4194336 | tf_op jit(solution)/shard_map/ppermute | solution.py:29
  290.1 1.9 copy-done.6
  292.1 4.0 collective-permute-start.3
  296.1 46.0 %collective-permute-done.3 = bf16[2,4,1024,256]{3,2,1,0:T(8,128)(2,1)} collective-permute-done((bf16[2,4,1024,256]{3,2,1,0:T(8,128)(2,1)S(1)}, bf16[2,4,1024,256]{3,2,1,0:T(8,128)(2,1)}, u32[]{:S(2)}, u32[]{:S(2)}) %collective-permute-start.3) | collective-permute-done | bytes 4194336 | tf_op jit(solution)/shard_map/ppermute | solution.py:29
  342.1 4.1 collective-permute-start.4
  346.4 0.6 fusion.51
  347.1 5.8 cholesky.17
  353.0 0.6 compare_reduce_fusion
  353.6 0.7 fusion.80
  354.3 4.9 custom-call.8
  359.5 0.4 fusion.50
  360.1 32.5 %collective-permute-done.4 = bf16[2,4,1024,256]{3,2,1,0:T(8,128)(2,1)} collective-permute-done((bf16[2,4,1024,256]{3,2,1,0:T(8,128)(2,1)}, bf16[2,4,1024,256]{3,2,1,0:T(8,128)(2,1)}, u32[]{:S(2)}, u32[]{:S(2)}) %collective-permute-start.4) | collective-permute-done | bytes 4194336 | tf_op jit(solution)/shard_map/ppermute | solution.py:29
  392.6 4.2 collective-permute-start.5
  396.8 4.8 copy_convert_fusion
  401.6 5.1 gather_fusion
  406.6 6.0 bitcast_convert_fusion.3
  412.7 5.1 gather_fusion.1
  417.7 6.6 %bitcast_convert_fusion.2 = f32[2,4,1024,256]{3,2,0,1:T(8,128)} fusion(bf16[4,2,1024,256]{3,2,1,0:T(8,128)(2,1)} %gather_fusion.1, pred[4]{0:T(512)(128)(4,1)S(1)} %get-tuple-element.31), kind=kLoop, calls=%fused_computation.7 | loop fusion | flops 4194304 | bytes 12582916 | tf_op jit(solution)/shard_map/convert_element_type | solution.py:48
  424.3 11.8 %multiply_add_fusion.3 = (f32[1,4,1024,256]{3,2,0,1:T(8,128)}, f32[1,4,1024,256]{3,2,0,1:T(8,128)}, f32[1,4,1024,256]{3,2,0,1:T(8,128)}, f32[1,4,1024,256]{3,2,0,1:T(8,128)}) fusion(f32[2,4,1024,256]{3,2,0,1:T(8,128)S(1)} %copy-done.1, f32[2,4,1024,256]{3,2,0,1:T(8,128)} %copy_convert_fusion, f32[2,4,1024,256]{3,2,0,1:T(8,128)} %bitcast_convert_fusion.2), kind=kLoop, calls=%fused_computation.16 | loop fusion | flops 12582912 | bytes 41943040 | tf_op jit(solution)/shard_map/add | solution.py:49
  436.1 5.2 sub.95
  441.3 5.2 add.191
  446.5 6.5 %fusion.40 = f32[4,256,64]{1,2,0:T(8,128)S(1)} fusion(f32[4,256,1024]{2,1,0:T(8,128)} %sub.95, s32[1024]{0:T(1024)S(1)} %add_select_fusion), kind=kOutput, calls=%fused_computation.66 | convolution fusion | flops 805437440 | bytes 4460544 | tf_op jit(solution)/shard_map/cbk,kp->cbp/dot_general | solution.py:60
  453.0 4.2 fusion.9
  457.4 0.3 stack_reshape.16
  457.8 5.2 sub.98
  463.0 5.5 add.194
  468.5 6.5 %fusion.37 = f32[4,256,64]{1,2,0:T(8,128)S(1)} fusion(f32[4,256,1024]{2,1,0:T(8,128)} %sub.98, s32[1024]{0:T(1024)S(1)} %add_select_fusion), kind=kOutput, calls=%fused_computation.63 | convolution fusion | flops 805437440 | bytes 4460544 | tf_op jit(solution)/shard_map/cbk,kp->cbp/dot_general | solution.py:60
  475.0 4.2 fusion.13
  479.8 5.0 gather_fusion.2
  484.8 6.0 bitcast_convert_fusion.1
  490.8 4.9 gather_fusion.3
  495.7 6.6 %bitcast_convert_fusion = f32[2,4,1024,256]{3,2,0,1:T(8,128)} fusion(bf16[4,2,1024,256]{3,2,1,0:T(8,128)(2,1)} %gather_fusion.3, pred[4]{0:T(512)(128)(4,1)S(1)} %get-tuple-element.29), kind=kLoop, calls=%fused_computation.5 | loop fusion | flops 4194304 | bytes 12582916 | tf_op jit(solution)/shard_map/convert_element_type | solution.py:48
  502.3 11.8 %multiply_add_fusion.1 = (f32[1,4,1024,256]{3,2,0,1:T(8,128)}, f32[1,4,1024,256]{3,2,0,1:T(8,128)}, f32[1,4,1024,256]{3,2,0,1:T(8,128)}, f32[1,4,1024,256]{3,2,0,1:T(8,128)}) fusion(f32[2,4,1024,256]{3,2,0,1:T(8,128)S(1)} %copy-done, f32[2,4,1024,256]{3,2,0,1:T(8,128)} %copy_convert_fusion, f32[2,4,1024,256]{3,2,0,1:T(8,128)} %bitcast_convert_fusion), kind=kLoop, calls=%fused_computation.12 | loop fusion | flops 12582912 | bytes 41943040 | tf_op jit(solution)/shard_map/add | solution.py:49
  514.1 5.3 sub.100
  519.4 6.3 fusion.34
  525.8 5.2 add.197
  530.9 6.4 %fusion.17 = f32[4,256,64]{1,2,0:T(8,128)S(1)} fusion(f32[4,256,64]{1,2,0:T(8,128)S(1)} %fusion.34, f32[4,256,1024]{2,1,0:T(8,128)} %add.197, s32[1024]{0:T(1024)S(1)} %add_select_fusion), kind=kOutput, calls=%fused_computation.43 | convolution fusion | flops 805765120 | bytes 4722688 | tf_op jit(solution)/shard_map/cbk,kp->cbp/dot_general | solution.py:53
  537.9 5.2 sub.102
  543.0 6.3 fusion.31
  549.4 5.3 add.200
  554.7 6.4 %fusion.21 = f32[4,256,64]{1,2,0:T(8,128)S(1)} fusion(f32[4,256,64]{1,2,0:T(8,128)S(1)} %fusion.31, f32[4,256,1024]{2,1,0:T(8,128)} %add.200, s32[1024]{0:T(1024)S(1)} %add_select_fusion), kind=kOutput, calls=%fused_computation.47 | convolution fusion | flops 805765120 | bytes 4722688 | tf_op jit(solution)/shard_map/cbk,kp->cbp/dot_general | solution.py:53
  561.6 2.0 fusion.22
  563.7 0.4 reshape.184
  564.0 5.1 fusion.86
  569.1 62.8 %reduce-scatter.2.cloned.1.call-done = f32[1024,64]{0,1:T(8,128)} async-done(((f32[16384,64]{0,1:T(8,128)}), f32[1024,64]{0,1:T(8,128)}) %reduce-scatter.2.cloned.1.call-update) | async-done | bytes 262160 | tf_op jit(solution)/shard_map/reduce_scatter | solution.py:125
  (63 shorter events, 2.6 us)
Async XLA Ops:
  6.5 625.4 %reduce-scatter.2.cloned.1.call-start = ((), (), s32[]{:S(2)}) async-start(), calls=%async_computation.1 | async-start | bytes 4456448 | tf_op jit(solution)/shard_map/reduce_scatter | solution.py:125
  7.6 179.5 %collective-permute-start = (bf16[2,4,63,256]{3,2,1,0:T(8,128)(2,1)S(1)}, bf16[2,4,63,256]{3,2,1,0:T(8,128)(2,1)S(1)}, u32[]{:S(2)}, u32[]{:S(2)}) collective-permute-start(bf16[2,4,63,256]{3,2,1,0:T(8,128)(2,1)S(1)} %get-tuple-element.26), channel_id=1, source_target_pairs={{0,16},{16,32},{32,48},{48,64},{64,80},{80,96},{96,112},{1,17},{17... | collective-permute-start | bytes 774152 | tf_op jit(solution)/shard_map/ppermute | solution.py:20
  11.5 175.7 %collective-permute-start.1 = (bf16[2,4,63,256]{3,2,1,0:T(8,128)(2,1)S(1)}, bf16[2,4,63,256]{3,2,1,0:T(8,128)(2,1)S(1)}, u32[]{:S(2)}, u32[]{:S(2)}) collective-permute-start(bf16[2,4,63,256]{3,2,1,0:T(8,128)(2,1)S(1)} %get-tuple-element.25), channel_id=1, source_target_pairs={{16,0},{32,16},{48,32},{64,48},{80,64},{96,80},{112,96},{17,1},{33... | collective-permute-start | bytes 774152 | tf_op jit(solution)/shard_map/ppermute | solution.py:21
  187.2 35.1 %slice-start = ((s8[9437184]{0:T(1024)(128)(4,1)}), s8[1048576]{0:T(1024)(128)(4,1)S(1)}, s32[]{:S(2)}) async-start(s8[9437184]{0:T(1024)(128)(4,1)} %bitcast.105), calls=%async_computation.2 | async-start | bytes 2097152
  212.9 9.4 %slice-start.1 = ((s8[9437184]{0:T(1024)(128)(4,1)}), s8[4194304]{0:T(1024)(128)(4,1)S(1)}, s32[]{:S(2)}) async-start(s8[9437184]{0:T(1024)(128)(4,1)} %bitcast.105), calls=%async_computation.3 | async-start | bytes 8388608
  212.9 9.4 %slice-start.2 = ((s8[9437184]{0:T(1024)(128)(4,1)}), s8[4194304]{0:T(1024)(128)(4,1)S(1)}, s32[]{:S(2)}) async-start(s8[9437184]{0:T(1024)(128)(4,1)} %bitcast.105), calls=%async_computation.4 | async-start | bytes 8388608
  212.9 9.4 %copy-start.5 = (bf16[2,4,1150,256]{3,2,1,0:T(8,128)(2,1)S(1)}, bf16[2,4,1150,256]{3,2,1,0:T(8,128)(2,1)}, u32[]{:S(2)}) copy-start(bf16[2,4,1150,256]{3,2,1,0:T(8,128)(2,1)} %concatenate.7) | copy-start | bytes 14131204
  222.3 13.0 %slice-start.3 = ((s8[9437184]{0:T(1024)(128)(4,1)}), s8[4194304]{0:T(1024)(128)(4,1)S(1)}, s32[]{:S(2)}) async-start(s8[9437184]{0:T(1024)(128)(4,1)} %bitcast.107), calls=%async_computation.5 | async-start | bytes 8388608
  222.3 13.0 %slice-start.4 = ((s8[9437184]{0:T(1024)(128)(4,1)}), s8[4194304]{0:T(1024)(128)(4,1)S(1)}, s32[]{:S(2)}) async-start(s8[9437184]{0:T(1024)(128)(4,1)} %bitcast.107), calls=%async_computation.6 | async-start | bytes 8388608
  226.7 8.6 %slice-start.5 = ((s8[9437184]{0:T(1024)(128)(4,1)}), s8[1048576]{0:T(1024)(128)(4,1)S(1)}, s32[]{:S(2)}) async-start(s8[9437184]{0:T(1024)(128)(4,1)} %bitcast.107), calls=%async_computation.7 | async-start | bytes 2097152
  226.7 8.6 %copy-start.8 = (f32[4,1024,256]{2,1,0:T(8,128)S(1)}, f32[4,1024,256]{2,1,0:T(8,128)}, u32[]{:S(2)}) copy-start(f32[4,1024,256]{2,1,0:T(8,128)} %fusion.2) | copy-start | bytes 12582916
  240.2 1.3 copy-start.4
  240.3 106.0 %copy-start.7 = (s32[256,2]{0,1:T(2,128)S(1)}, s32[256,2]{0,1:T(2,128)}, u32[]{:S(2)}) copy-start(s32[256,2]{0,1:T(2,128)} %param.7) | copy-start | bytes 6148
  241.6 48.6 %collective-permute-start.2 = (bf16[2,4,1024,256]{3,2,1,0:T(8,128)(2,1)S(1)}, bf16[2,4,1024,256]{3,2,1,0:T(8,128)(2,1)S(1)}, u32[]{:S(2)}, u32[]{:S(2)}) collective-permute-start(bf16[2,4,1024,256]{3,2,1,0:T(8,128)(2,1)S(1)} %pad_maximum_fusion), channel_id=1, source_target_pairs={{0,15},{1,0},{2,1},{3,2},{4,3},{5,4},{6,5},{7,6},{8,7},{9,8},{10,9... | collective-permute-start | bytes 12582920 | tf_op jit(solution)/shard_map/ppermute | solution.py:29
  290.1 1.9 copy-start.6
  292.1 50.0 %collective-permute-start.3 = (bf16[2,4,1024,256]{3,2,1,0:T(8,128)(2,1)S(1)}, bf16[2,4,1024,256]{3,2,1,0:T(8,128)(2,1)}, u32[]{:S(2)}, u32[]{:S(2)}) collective-permute-start(bf16[2,4,1024,256]{3,2,1,0:T(8,128)(2,1)S(1)} %collective-permute-done.2), channel_id=1, source_target_pairs={{0,15},{1,0},{2,1},{3,2},{4,3},{5,4},{6,5},{7,6},{8,7},{9,8},{10,9... | collective-permute-start | bytes 12582920 | tf_op jit(solution)/shard_map/ppermute | solution.py:29
  342.1 50.5 %collective-permute-start.4 = (bf16[2,4,1024,256]{3,2,1,0:T(8,128)(2,1)}, bf16[2,4,1024,256]{3,2,1,0:T(8,128)(2,1)}, u32[]{:S(2)}, u32[]{:S(2)}) collective-permute-start(bf16[2,4,1024,256]{3,2,1,0:T(8,128)(2,1)} %collective-permute-done.3), channel_id=1, source_target_pairs={{0,15},{1,0},{2,1},{3,2},{4,3},{5,4},{6,5},{7,6},{8,7},{9,8},{10,9... | collective-permute-start | bytes 12582920 | tf_op jit(solution)/shard_map/ppermute | solution.py:29
  392.6 98.2 %collective-permute-start.5 = (bf16[2,4,1024,256]{3,2,1,0:T(8,128)(2,1)}, bf16[2,4,1024,256]{3,2,1,0:T(8,128)(2,1)}, u32[]{:S(2)}, u32[]{:S(2)}) collective-permute-start(bf16[2,4,1024,256]{3,2,1,0:T(8,128)(2,1)} %collective-permute-done.4), channel_id=1, source_target_pairs={{0,15},{1,0},{2,1},{3,2},{4,3},{5,4},{6,5},{7,6},{8,7},{9,8},{10,9... | collective-permute-start | bytes 12582920 | tf_op jit(solution)/shard_map/ppermute | solution.py:29
  417.7 6.6 %copy-start.1 = (f32[2,4,1024,256]{3,2,0,1:T(8,128)S(1)}, f32[2,4,1024,256]{3,2,0,1:T(8,128)}, u32[]{:S(2)}) copy-start(f32[2,4,1024,256]{3,2,0,1:T(8,128)} %bitcast_convert_fusion.3) | copy-start | bytes 25165828
  446.5 6.5 %copy-start.2 = (f32[4,256,1024]{2,1,0:T(8,128)S(1)}, f32[4,256,1024]{2,1,0:T(8,128)}, u32[]{:S(2)}) copy-start(f32[4,256,1024]{2,1,0:T(8,128)} %add.191) | copy-start | bytes 12582916
  468.5 6.5 %copy-start.3 = (f32[4,256,1024]{2,1,0:T(8,128)S(1)}, f32[4,256,1024]{2,1,0:T(8,128)}, u32[]{:S(2)}) copy-start(f32[4,256,1024]{2,1,0:T(8,128)} %add.194) | copy-start | bytes 12582916
  495.7 6.6 %copy-start = (f32[2,4,1024,256]{3,2,0,1:T(8,128)S(1)}, f32[2,4,1024,256]{3,2,0,1:T(8,128)}, u32[]{:S(2)}) copy-start(f32[2,4,1024,256]{3,2,0,1:T(8,128)} %bitcast_convert_fusion.1) | copy-start | bytes 25165828
Sparse Core Ops, SparseCore 0:
  569.2 62.6 reduce-scatter.1
where the time goes:
time: 649 us; the launch traced here: 639 us
  local copies, waits for them, and re-layouts  264 us (41%)
  waiting for transfers between devices  187 us (29%)
  matrix products  82.4 us (13%)
  other arithmetic  66.3 us (10%)
  starting transfers between devices  24.3 us (4%)
  between operations  14.1 us (2%)
    ppermute x4, waiting for transfers between devices, from_behind(): return lax.ppermute(value, axis, pairs)  125 us
    reduce_scatter x1, waiting for transfers between devices, per_device(): lax.psum_scatter(lax.dot_general(pair_phase, own_map, (((0,), (1,)), ((),...  62.8 us
    another operation x2, local copies, waits for them, and re-layouts, band_matrix(): tiled = jnp.tile(line, (1,) * len(lead) + (rows,))  61.3 us
    unnamed x32, local copies, waits for them, and re-layouts  50.8 us
    squeeze x2, local copies, waits for them, and re-layouts, per_device(): real_part = convolve(matrix[0], padded[0]) - convolve(matrix[1], padded[1])  41.3 us
    dot_general x4, matrix products, convolve(): jnp.einsum('arl,alg->arg', taps_part, image_part, preferred_element_type=...  27.3 us
    dot_general x4, matrix products, linear_phase(): jnp.einsum('cbk,kp->cbp', imag.reshape(count, rows // LOOK, LOOK * column...  25.7 us
    concatenate x1, local copies, waits for them, and re-layouts, extended(): array = jnp.concatenate([before, array, after], axis=dim)  25.7 us
  transfers between devices with their start and end apart: 7, of which 4 were waited for; matrix products, arithmetic and copies ran while one was open for 43% of the time, Pallas kernels for 0%

commit v1 on v0

v1 whole, which is shorter than its diff:
```python
import jax
import jax.numpy as jnp
from jax import lax
from jax.experimental import pallas as pl
from jax.experimental.pallas import tpu as pltpu
from jax.sharding import PartitionSpec as P

LOOK = 4
REACH = 4
BLOCK = 128
CHUNK = 64
HALO = 64
RIDGE = 1.0
MIB = 1 << 20


def column_order(columns):
    source = lax.broadcasted_iota(jnp.int32, (columns, columns), 0)
    target = lax.broadcasted_iota(jnp.int32, (columns, columns), 1)
    looked = columns // LOOK
    wanted = (target % looked) * LOOK + target // looked
    return jnp.where(source == wanted, 1.0, 0.0).astype(jnp.bfloat16)


def fill_bands(taps_ref, band_ref, a):
    lines = [jnp.broadcast_to(taps_ref[part, a : a + 1, :], (8, 2 * BLOCK)) for part in range(2)]
    for m in range(0, BLOCK, 16):
        chunk, look = m // CHUNK, m % CHUNK // 16
        pieces = []
        for part in range(2):
            halves = [
                pltpu.roll(
                    lines[part], chunk * CHUNK + look + LOOK * half + 1, 1, stride=2 * LOOK, stride_axis=0
                )
                for half in range(2)
            ]
            pieces.append(jnp.concatenate(halves, axis=0))
        real, imag = pieces
        band_ref[0, m : m + 16, :] = real.astype(jnp.bfloat16)
        band_ref[0, BLOCK + m : BLOCK + m + 16, :] = imag.astype(jnp.bfloat16)
        band_ref[1, m : m + 16, :] = (-imag).astype(jnp.bfloat16)
        band_ref[1, BLOCK + m : BLOCK + m + 16, :] = real.astype(jnp.bfloat16)


def filter_block(band, first, second):
    both = jnp.dot(band[0], first, preferred_element_type=jnp.float32)
    both += jnp.dot(band[1], second, preferred_element_type=jnp.float32)
    return both.astype(jnp.bfloat16)


def interior_kernel(taps_ref, image_ref, out_ref, band_out_ref, ordered):
    a = pl.program_id(0)
    rows = image_ref.shape[2]
    order = column_order(image_ref.shape[3])
    for acq in range(taps_ref.shape[1]):

        @pl.when(a == acq)
        def _():
            fill_bands(taps_ref, band_out_ref.at[0], acq)

    for part in range(2):
        ordered[part] = jnp.dot(
            image_ref[part, 0], order, preferred_element_type=jnp.float32
        ).astype(jnp.bfloat16)
    band = band_out_ref[0]
    for block in range(1, rows // BLOCK - 1):
        window = pl.ds(block * BLOCK - HALO, 2 * BLOCK)
        both = filter_block(band, ordered[0, window, :], ordered[1, window, :])
        for chunk in range(2):
            for part in range(2):
                start = part * BLOCK + chunk * CHUNK
                out_ref[2 * block + chunk, part, 0] = both[start : start + CHUNK]


def edge_kernel(band_ref, inner_ref, halo_ref, filled_ref, out_ref):
    del filled_ref
    e = pl.program_id(0)
    order = column_order(inner_ref.shape[4])
    for acq in range(inner_ref.shape[2]):
        band = band_ref[acq]

        def put(windows):
            parts = [
                jnp.dot(w, order, preferred_element_type=jnp.float32).astype(jnp.bfloat16) for w in windows
            ]
            both = filter_block(band, parts[0], parts[1])
            for chunk in range(2):
                for part in range(2):
                    start = part * BLOCK + chunk * CHUNK
                    out_ref[chunk, part, acq] = both[start : start + CHUNK]

        @pl.when(e == 0)
        def _():
            put([jnp.concatenate([halo_ref[0, p, acq], inner_ref[0, p, acq]], axis=0) for p in range(2)])

        @pl.when(e == 1)
        def _():
            put([jnp.concatenate([inner_ref[0, p, acq], halo_ref[0, p, acq]], axis=0) for p in range(2)])


def pair_kernel(second_ref, map_ref, got_ref, out_ref, image, phase):
    groups, _, slots = got_ref.shape[:3]

    def widen(g, carry):
        for slot in range(slots):
            for part in range(2):
                image[part, g * slots + slot] = got_ref[g, part, slot].astype(jnp.float32)
        return carry

    lax.fori_loop(0, groups, widen, 0)
    lane = lax.broadcasted_iota(jnp.int32, (8, 128), 1)
    low = lane < 64

    def fold(value):
        upper, lower = value[:8], value[8:]
        return jnp.where(low, upper, lower) + pltpu.roll(jnp.where(low, lower, upper), 64, 1)

    def one_reference(i, carry):
        others = [second_ref[i * REACH + j] for j in range(REACH)]
        real = [None] * REACH
        imag = [None] * REACH
        for look in range(LOOK):
            for side in range(2):
                where = (pl.ds(look * 16, 16), pl.ds(side * 128, 128))
                a_re, a_im = (image[part, i, where[0], where[1]] for part in range(2))
                for j, k in enumerate(others):
                    b_re, b_im = (image[part, k, where[0], where[1]] for part in range(2))
                    re = a_re * b_re + a_im * b_im
                    im = a_im * b_re - a_re * b_im
                    real[j] = re if real[j] is None else real[j] + re
                    imag[j] = im if imag[j] is None else imag[j] + im
        for j in range(REACH):
            re, im = fold(real[j]), fold(imag[j])
            least = float(LOOK**4)
            ratio = im * lax.rsqrt(jnp.maximum(re * re + im * im, least))
            phase[pl.ds(pl.multiple_of((i * REACH + j) * 8, 8), 8), :] = ratio
        return carry

    lax.fori_loop(0, groups * slots, one_reference, 0)

    table = map_ref[...]
    acqs, pairs = table.shape
    high = table.astype(jnp.bfloat16)
    rest = (table - high.astype(jnp.float32)).astype(jnp.bfloat16)
    stacked = jnp.concatenate([high, rest], axis=0)
    for t in range(8):
        value = phase[pl.ds(t, pairs, stride=8), :]
        v_high = value.astype(jnp.bfloat16)
        v_rest = (value - v_high.astype(jnp.float32)).astype(jnp.bfloat16)
        both = jnp.dot(stacked, v_high, preferred_element_type=jnp.float32)
        total = both[:acqs] + both[acqs:] + jnp.dot(high, v_rest, preferred_element_type=jnp.float32)
        out_ref[:, t * 128 : (t + 1) * 128] = total


def inverse_of(pair_list, total_acq):
    labels = jnp.arange(total_acq, dtype=jnp.int32)
    incidence = (pair_list[:, 1:2] == labels).astype(jnp.float32) - (pair_list[:, 0:1] == labels).astype(jnp.float32)
    normal = jnp.dot(
        incidence.T, incidence, precision=lax.Precision.HIGHEST, preferred_element_type=jnp.float32
    ) + RIDGE * jnp.eye(total_acq, dtype=jnp.float32)
    lower = jnp.linalg.cholesky(normal)
    partial_solve = lax.linalg.triangular_solve(lower, incidence.T, left_side=True, lower=True)
    return lax.linalg.triangular_solve(lower, partial_solve, left_side=True, lower=True, transpose_a=True)


def per_device(radar_stack, band_taps, pair_list):
    groups = lax.axis_size("acq")
    blocks_az = lax.axis_size("az")
    _, local, rows, columns = radar_stack.shape
    up = [(i, i + 1) for i in range(blocks_az - 1)]
    down = [(j, i) for i, j in up]
    before = lax.ppermute(radar_stack[:, :, rows - HALO :], "az", up)
    after = lax.ppermute(radar_stack[:, :, :HALO], "az", down)
    taps = jnp.pad(band_taps.astype(jnp.float32), ((0, 0), (0, 0), (0, 2 * BLOCK - band_taps.shape[2])))

    filtered, band = pl.pallas_call(
        interior_kernel,
        grid=(local,),
        in_specs=[
            pl.BlockSpec((2, local, 2 * BLOCK), lambda a: (0, 0, 0)),
            pl.BlockSpec((2, 1, rows, columns), lambda a: (0, a, 0, 0)),
        ],
        out_specs=[
            pl.BlockSpec((groups, 2, 1, CHUNK, columns), lambda a: (0, 0, a, 0, 0)),
            pl.BlockSpec((1, 2, 2 * BLOCK, 2 * BLOCK), lambda a: (a, 0, 0, 0)),
        ],
        out_shape=[
            jax.ShapeDtypeStruct((groups, 2, local, CHUNK, columns), jnp.bfloat16),
            jax.ShapeDtypeStruct((local, 2, 2 * BLOCK, 2 * BLOCK), jnp.bfloat16),
        ],
        scratch_shapes=[pltpu.VMEM((2, rows, columns), jnp.bfloat16)],
        compiler_params=pltpu.CompilerParams(vmem_limit_bytes=40 * MIB),
        cost_estimate=pl.CostEstimate(flops=3_000_000_000, bytes_accessed=9_000_000, transcendentals=0),
        name="filter_interior",
    )(taps, radar_stack)

    near = 2 * BLOCK - HALO
    inner = jnp.stack([radar_stack[:, :, :near], radar_stack[:, :, rows - near :]])
    halo = jnp.stack([before, after])
    last = groups // 2 - 1
    filtered = pl.pallas_call(
        edge_kernel,
        grid=(2,),
        in_specs=[
            pl.BlockSpec((local, 2, 2 * BLOCK, 2 * BLOCK), lambda e: (0, 0, 0, 0)),
            pl.BlockSpec((1, 2, local, near, columns), lambda e: (e, 0, 0, 0, 0)),
            pl.BlockSpec((1, 2, local, HALO, columns), lambda e: (e, 0, 0, 0, 0)),
            pl.BlockSpec(memory_space=pl.ANY),
        ],
        out_specs=pl.BlockSpec((2, 2, local, CHUNK, columns), lambda e: (e * last, 0, 0, 0, 0)),
        out_shape=jax.ShapeDtypeStruct(filtered.shape, filtered.dtype),
        input_output_aliases={3: 0},
        compiler_params=pltpu.CompilerParams(vmem_limit_bytes=40 * MIB),
        cost_estimate=pl.CostEstimate(flops=900_000_000, bytes_accessed=5_000_000, transcendentals=0),
        name="filter_edges",
    )(band, inner, halo, filtered)

    got = lax.all_to_all(filtered, "acq", 0, 0, tiled=True)
    inverse_map = inverse_of(pair_list, groups * local)

    return pl.pallas_call(
        pair_kernel,
        in_specs=[
            pl.BlockSpec(memory_space=pltpu.SMEM),
            pl.BlockSpec(memory_space=pltpu.VMEM),
            pl.BlockSpec(memory_space=pltpu.VMEM),
        ],
        out_specs=pl.BlockSpec(memory_space=pltpu.VMEM),
        out_shape=jax.ShapeDtypeStruct((groups * local, CHUNK // LOOK * columns // LOOK), jnp.float32),
        scratch_shapes=[
            pltpu.VMEM((2, groups * local, CHUNK, columns), jnp.float32),
            pltpu.VMEM((pair_list.shape[0] * 8, 128), jnp.float32),
        ],
        compiler_params=pltpu.CompilerParams(vmem_limit_bytes=40 * MIB),
        cost_estimate=pl.CostEstimate(flops=100_000_000, bytes_accessed=5_000_000, transcendentals=300_000),
        name="pairs_and_inversion",
    )(pair_list[:, 1], inverse_map, got)


def solution(mesh):
    return jax.shard_map(
        per_device,
        mesh=mesh,
        in_specs=(P(None, "acq", "az", None), P(None, "acq", None), P()),
        out_specs=P(None, ("az", "acq")),
        check_vma=False,
    )
```

time: 649 us -> 106 us (0.16)
  the two profiles are of different devices: /device:TPU:4 before, /device:TPU:123 now
where the time goes in v1:
time: 106 us; the launch traced here: 105 us
  waiting for transfers between devices  51.6 us (49%)
  Pallas kernels  22.7 us (21%)
  starting transfers between devices  12.7 us (12%)
  other arithmetic  12.3 us (12%)
  local copies, waits for them, and re-layouts  4.78 us (5%)
  matrix products  1.15 us (1%)
    all_to_all x1, waiting for transfers between devices, per_device(): got = lax.all_to_all(filtered, 'acq', 0, 0, tiled=True)  48.4 us
    pallas_call x1, Pallas kernels, per_device(): pl.pallas_call(pair_kernel, in_specs=[pl.BlockSpec(memory_space=pltpu.SME...  13.6 us
    all_to_all x1, starting transfers between devices, per_device(): got = lax.all_to_all(filtered, 'acq', 0, 0, tiled=True)  7.25 us
    another operation x3, other arithmetic, inverse_of(): lower = jnp.linalg.cholesky(normal)  6.52 us
    another operation x2, other arithmetic, inverse_of(): lax.linalg.triangular_solve(lower, partial_solve, left_side=True, lower=T...  5.55 us
    pallas_call x1, Pallas kernels, per_device(): pl.pallas_call(interior_kernel, grid=(local,), in_specs=[pl.BlockSpec((2,...  4.57 us
    pallas_call x1, Pallas kernels, per_device(): pl.pallas_call(edge_kernel, grid=(2,), in_specs=[pl.BlockSpec((local, 2,...  4.53 us
    ppermute x1, waiting for transfers between devices, per_device(): after = lax.ppermute(radar_stack[:, :, :HALO], 'az', down)  3.18 us
  transfers between devices with their start and end apart: 3, of which 2 were waited for; matrix products, arithmetic and copies ran while one was open for 14% of the time, Pallas kernels for 4%

profile of v1, /device:TPU:123, one launch (start us, length us, event | category | flops | bytes accessed | tf_op | source)
XLA Modules:
  0.0 105.4 jit_solution(13955433312651890256)
XLA Ops:
  0.0 0.0 copy-start.1
  0.0 0.0 copy-start.2
  0.0 1.2 %fusion.12 = (bf16[2,4,64,256]{3,2,1,0:T(8,128)(2,1)S(1)}, bf16[2,4,64,256]{3,2,1,0:T(8,128)(2,1)S(1)}) fusion(bf16[2,4,1024,256]{3,2,1,0:T(8,128)(2,1)} %image_ref.1), kind=kLoop, calls=%fused_computation.27 | loop fusion | bytes 1048576 | tf_op jit(solution)/shard_map/slice | solution.py:172
  1.2 2.5 %collective-permute-start = (bf16[2,4,64,256]{3,2,1,0:T(8,128)(2,1)S(1)}, bf16[2,4,64,256]{3,2,1,0:T(8,128)(2,1)S(1)}, u32[]{:S(2)}, u32[]{:S(2)}) collective-permute-start(bf16[2,4,64,256]{3,2,1,0:T(8,128)(2,1)S(1)} %get-tuple-element.9), channel_id=1, source_target_pairs={{0,16},{16,32},{32,48},{48,64},{64,80},{80,96},{96,112},{1,17},{17... | collective-permute-start | bytes 786440 | tf_op jit(solution)/shard_map/ppermute | solution.py:172
  3.8 2.9 %collective-permute-start.1 = (bf16[2,4,64,256]{3,2,1,0:T(8,128)(2,1)S(1)}, bf16[2,4,64,256]{3,2,1,0:T(8,128)(2,1)S(1)}, u32[]{:S(2)}, u32[]{:S(2)}) collective-permute-start(bf16[2,4,64,256]{3,2,1,0:T(8,128)(2,1)S(1)} %get-tuple-element.10), channel_id=1, source_target_pairs={{16,0},{32,16},{48,32},{64,48},{80,64},{96,80},{112,96},{17,1},{33... | collective-permute-start | bytes 786440 | tf_op jit(solution)/shard_map/ppermute | solution.py:173
  6.7 1.5 %slice_bitcast_fusion.1 = (bf16[1,2,4,192,256]{4,3,2,1,0:T(8,128)(2,1)S(1)}, bf16[1,2,4,192,256]{4,3,2,1,0:T(8,128)(2,1)S(1)}) fusion(bf16[2,4,1024,256]{3,2,1,0:T(8,128)(2,1)} %image_ref.1), kind=kLoop, calls=%fused_computation.2 | loop fusion | bytes 3145728 | tf_op jit(solution)/shard_map/stack | solution.py:198
  8.2 0.0 copy-done.2
  8.2 0.1 pad_maximum_fusion.inner_ref
  8.4 0.0 copy-done.1
  8.4 4.6 %filter_interior.1 = (bf16[16,2,4,64,256]{4,3,2,1,0:T(8,128)(2,1)S(1)}, bf16[4,2,256,256]{3,2,1,0:T(8,128)(2,1)S(1)}) custom-call(f32[2,4,256]{2,1,0:T(4,128)S(1)} %pad_convert_fusion.taps_ref, bf16[2,4,1024,256]{3,2,1,0:T(8,128)(2,1)S(1)} %copy-done.1), custom_call_target="tpu_custom_call" | custom-call | flops 3000000000 | bytes 9000000 | tf_op jit(solution)/shard_map/filter_interior/pallas_call | solution.py:176
  12.9 0.0 collective-permute-done
  13.0 3.2 %collective-permute-done.1 = bf16[2,4,64,256]{3,2,1,0:T(8,128)(2,1)S(1)} collective-permute-done((bf16[2,4,64,256]{3,2,1,0:T(8,128)(2,1)S(1)}, bf16[2,4,64,256]{3,2,1,0:T(8,128)(2,1)S(1)}, u32[]{:S(2)}, u32[]{:S(2)}) %collective-permute-start.1) | collective-permute-done | bytes 262176 | tf_op jit(solution)/shard_map/ppermute | solution.py:173
  16.1 0.1 pad_maximum_fusion.1.halo_ref
  16.2 4.5 %filter_edges.1 = bf16[16,2,4,64,256]{4,3,2,1,0:T(8,128)(2,1)S(1)} custom-call(bf16[4,2,256,256]{3,2,1,0:T(8,128)(2,1)S(1)} %get-tuple-element.7.band_ref, bf16[2,2,4,192,256]{4,3,2,1,0:T(8,128)(2,1)S(1)} %pad_maximum_fusion.inner_ref, bf16[2,2,4,64,256]{4,3,2,1,0:T(8,128)(2,1)S(1)} %pad_maximum_fusion.1.halo_ref, ...), custom_call_target="tpu_custom_call", output_to_operand_aliasing={{}: (3, {})} | custom-call | flops 900000000 | bytes 5000000 | tf_op jit(solution)/shard_map/filter_edges/pallas_call | solution.py:201
  20.7 0.0 copy-start
  20.7 2.0 %copy-done = bf16[16,2,4,64,256]{4,3,2,1,0:T(8,128)(2,1)} copy-done((bf16[16,2,4,64,256]{4,3,2,1,0:T(8,128)(2,1)}, bf16[16,2,4,64,256]{4,3,2,1,0:T(8,128)(2,1)S(1)}, u32[]{:S(2)}) %copy-start) | copy-done | bytes 4194328
  22.7 0.0 copy-start.3
  22.7 7.2 %all-to-all-start = ((bf16[16,2,4,64,256]{4,3,2,1,0:T(8,128)(2,1)}), bf16[16,2,4,64,256]{4,3,2,1,0:T(8,128)(2,1)}, u32[]{:S(2)}, u32[]{:S(2)}) async-start(bf16[16,2,4,64,256]{4,3,2,1,0:T(8,128)(2,1)} %copy-done), calls=%async_computation | async-start | bytes 8388608 | tf_op jit(solution)/shard_map/all_to_all | solution.py:218
  29.9 0.0 copy-done.3
  30.0 0.6 fusion.1
  30.5 0.1 copy.5
  30.6 5.8 %cholesky.17 = f32[64,64]{1,0:T(8,128)S(1)} custom-call(f32[64,64]{1,0:T(8,128)S(1)} %fusion.11), custom_call_target="Cholesky" | custom-call | tf_op jit(solution)/shard_map/jit(cholesky)/cholesky | solution.py:161
  36.5 0.6 compare_reduce_fusion
  37.2 0.7 fusion.6
  37.8 4.9 %custom-call.8 = f32[1,64,64]{1,2,0:T(8,128)S(1)} custom-call(f32[1,64,64]{2,1,0:T(8,128)S(1)} %fusion.6), custom_call_target="InvertDiagBlocksLowerTriangular" | custom-call | tf_op jit(solution)/shard_map/triangular_solve | solution.py:163
  42.7 0.4 fusion
  43.1 0.2 fusion.7.map_ref
  43.3 48.4 %all-to-all-done.got_ref = bf16[16,2,4,64,256]{4,3,2,1,0:T(8,128)(2,1)} async-done(((bf16[16,2,4,64,256]{4,3,2,1,0:T(8,128)(2,1)}), bf16[16,2,4,64,256]{4,3,2,1,0:T(8,128)(2,1)}, u32[]{:S(2)}, u32[]{:S(2)}) %all-to-all-start) | async-done | bytes 4194336 | tf_op jit(solution)/shard_map/all_to_all | solution.py:218
  91.8 13.6 %pairs_and_inversion.1 = f32[64,1024]{1,0:T(8,128)} custom-call(s32[256]{0:T(256)S(1)} %bitcast.24, f32[64,256]{1,0:T(8,128)S(1)} %fusion.7.map_ref, bf16[16,2,4,64,256]{4,3,2,1,0:T(8,128)(2,1)} %all-to-all-done.got_ref), custom_call_target="tpu_custom_call" | custom-call | flops 100000000 | bytes 5000000 | tf_op jit(solution)/shard_map/pairs_and_inversion/pallas_call | solution.py:221
  (4 shorter events, 0.1 us)
Async XLA Ops:
  0.0 8.4 %copy-start.1 = (bf16[2,4,1024,256]{3,2,1,0:T(8,128)(2,1)S(1)}, bf16[2,4,1024,256]{3,2,1,0:T(8,128)(2,1)}, u32[]{:S(2)}) copy-start(bf16[2,4,1024,256]{3,2,1,0:T(8,128)(2,1)} %image_ref.1) | copy-start | bytes 12582916
  0.0 8.2 %copy-start.2 = (bf16[2,4,127]{2,1,0:T(4,128)(2,1)S(1)}, bf16[2,4,127]{2,1,0:T(4,128)(2,1)}, u32[]{:S(2)}) copy-start(bf16[2,4,127]{2,1,0:T(4,128)(2,1)} %param.4) | copy-start | bytes 6100
  1.2 11.7 %collective-permute-start = (bf16[2,4,64,256]{3,2,1,0:T(8,128)(2,1)S(1)}, bf16[2,4,64,256]{3,2,1,0:T(8,128)(2,1)S(1)}, u32[]{:S(2)}, u32[]{:S(2)}) collective-permute-start(bf16[2,4,64,256]{3,2,1,0:T(8,128)(2,1)S(1)} %get-tuple-element.9), channel_id=1, source_target_pairs={{0,16},{16,32},{32,48},{48,64},{64,80},{80,96},{96,112},{1,17},{17... | collective-permute-start | bytes 786440 | tf_op jit(solution)/shard_map/ppermute | solution.py:172
  3.8 12.4 %collective-permute-start.1 = (bf16[2,4,64,256]{3,2,1,0:T(8,128)(2,1)S(1)}, bf16[2,4,64,256]{3,2,1,0:T(8,128)(2,1)S(1)}, u32[]{:S(2)}, u32[]{:S(2)}) collective-permute-start(bf16[2,4,64,256]{3,2,1,0:T(8,128)(2,1)S(1)} %get-tuple-element.10), channel_id=1, source_target_pairs={{16,0},{32,16},{48,32},{64,48},{80,64},{96,80},{112,96},{17,1},{33... | collective-permute-start | bytes 786440 | tf_op jit(solution)/shard_map/ppermute | solution.py:173
  20.7 2.0 %copy-start = (bf16[16,2,4,64,256]{4,3,2,1,0:T(8,128)(2,1)}, bf16[16,2,4,64,256]{4,3,2,1,0:T(8,128)(2,1)S(1)}, u32[]{:S(2)}) copy-start(bf16[16,2,4,64,256]{4,3,2,1,0:T(8,128)(2,1)S(1)} %filter_edges.1) | copy-start | bytes 12582916
  22.7 7.3 %copy-start.3 = (s32[256,2]{0,1:T(2,128)S(1)}, s32[256,2]{0,1:T(2,128)}, u32[]{:S(2)}) copy-start(s32[256,2]{0,1:T(2,128)} %param.5) | copy-start | bytes 6148
  22.7 69.1 %all-to-all-start = ((bf16[16,2,4,64,256]{4,3,2,1,0:T(8,128)(2,1)}), bf16[16,2,4,64,256]{4,3,2,1,0:T(8,128)(2,1)}, u32[]{:S(2)}, u32[]{:S(2)}) async-start(bf16[16,2,4,64,256]{4,3,2,1,0:T(8,128)(2,1)} %copy-done), calls=%async_computation | async-start | bytes 8388608 | tf_op jit(solution)/shard_map/all_to_all | solution.py:218

commit v2 on v1

v2 whole, which is shorter than its diff:
```python
import jax
import jax.numpy as jnp
from jax import lax
from jax.experimental import pallas as pl
from jax.experimental.pallas import tpu as pltpu
from jax.sharding import PartitionSpec as P

LOOK = 4
REACH = 4
BLOCK = 128
CHUNK = 64
HALO = 64
REST = 2 * BLOCK - HALO
CORES = 2
SOLVER_STEPS = 3
RIDGE = 1.0
MIB = 1 << 20
VMEM = pl.BlockSpec(memory_space=pltpu.VMEM)
SMEM = pl.BlockSpec(memory_space=pltpu.SMEM)
HBM = pl.BlockSpec(memory_space=pltpu.HBM)


def column_order(columns):
    source = lax.broadcasted_iota(jnp.int32, (columns, columns), 0)
    target = lax.broadcasted_iota(jnp.int32, (columns, columns), 1)
    looked = columns // LOOK
    wanted = (target % looked) * LOOK + target // looked
    return jnp.where(source == wanted, 1.0, 0.0).astype(jnp.bfloat16)


def fill_bands(taps_ref, band_ref, a):
    lines = [jnp.broadcast_to(taps_ref[part, a : a + 1, :], (8, 2 * BLOCK)) for part in range(2)]
    for m in range(0, BLOCK, 16):
        chunk, look = m // CHUNK, m % CHUNK // 16
        pieces = []
        for part in range(2):
            halves = [
                pltpu.roll(
                    lines[part], chunk * CHUNK + look + LOOK * half + 1, 1, stride=2 * LOOK, stride_axis=0
                )
                for half in range(2)
            ]
            pieces.append(jnp.concatenate(halves, axis=0))
        real, imag = pieces
        band_ref[0, m : m + 16, :] = real.astype(jnp.bfloat16)
        band_ref[0, BLOCK + m : BLOCK + m + 16, :] = imag.astype(jnp.bfloat16)
        band_ref[1, m : m + 16, :] = (-imag).astype(jnp.bfloat16)
        band_ref[1, BLOCK + m : BLOCK + m + 16, :] = real.astype(jnp.bfloat16)


def place_of(group_ref):
    group = group_ref[0]
    return group // (CHIPS * CORES), group // CORES % CHIPS, group % CORES


def elimination(pairs_ref, map_ref):
    total = map_ref.shape[0]
    label = lax.broadcasted_iota(jnp.int32, map_ref.shape, 0)
    incidence = jnp.where(label == pairs_ref[1:2, :], 1.0, 0.0) - jnp.where(label == pairs_ref[0:1, :], 1.0, 0.0)
    exact = incidence.astype(jnp.bfloat16)
    normal = lax.dot_general(exact, exact, (((1,), (1,)), ((), ())), preferred_element_type=jnp.float32)
    row = lax.broadcasted_iota(jnp.int32, (total, total), 0)
    column = lax.broadcasted_iota(jnp.int32, (total, total), 1)
    unit = jnp.where(row == column, 1.0, 0.0)
    table = jnp.concatenate([normal + RIDGE * unit, unit], axis=1)
    index = lax.broadcasted_iota(jnp.int32, table.shape, 0)
    for k in range(total):
        scaled = table[k : k + 1, :] * (1.0 / table[k : k + 1, k : k + 1])
        table = jnp.where(index == k, scaled, table - table[:, k : k + 1] * scaled)
        yield
    map_ref[...] = jnp.dot(
        table[:, total:], incidence, precision=lax.Precision.HIGHEST, preferred_element_type=jnp.float32
    )


def filter_window(band_ref, a, windows):
    both = jnp.dot(band_ref[a, 0], windows[0], preferred_element_type=jnp.float32)
    both += jnp.dot(band_ref[a, 1], windows[1], preferred_element_type=jnp.float32)
    return both.astype(jnp.bfloat16)


def interior_kernel(
    taps_ref, pairs_ref, image_ref, out_ref, band_ref, edge_ref, map_ref, image, ordered, done, arrived, left
):
    _, local, rows, columns = image.shape
    blocks = rows // BLOCK
    inward = [pltpu.make_async_copy(image_ref.at[:, a], image.at[:, a], arrived.at[a]) for a in range(local)]
    inner = pl.ds(CORES, CORES * (blocks - 2))
    outward = [pltpu.make_async_copy(done.at[a], out_ref.at[inner, :, a], left.at[a]) for a in range(local)]
    for copy in inward:
        copy.start()
    order = column_order(columns)
    solver = elimination(pairs_ref, map_ref)
    for a in range(local):
        fill_bands(taps_ref, band_ref.at[a], a)
        inward[a].wait()
        for part in range(2):
            ordered[part] = jnp.dot(image[part, a], order, preferred_element_type=jnp.float32).astype(jnp.bfloat16)
            edge_ref[0, part, a] = ordered[part, :REST, :]
            edge_ref[1, part, a] = ordered[part, rows - REST :, :]
        for block in range(1, blocks - 1):
            window = pl.ds(block * BLOCK - HALO, 2 * BLOCK)
            both = filter_window(band_ref, a, [ordered[part, window, :] for part in range(2)])
            for core in range(CORES):
                for part in range(2):
                    start = part * BLOCK + core * CHUNK
                    done[a, (block - 1) * CORES + core, part] = both[start : start + CHUNK]
            for _ in range(SOLVER_STEPS):
                next(solver, None)
        outward[a].start()
    for _ in solver:
        pass
    for copy in outward:
        copy.wait()


def edge_kernel(band_ref, edge_ref, before_ref, after_ref, filled_ref, out_ref, done, left):
    del filled_ref
    local, columns = before_ref.shape[1], before_ref.shape[3]
    order = column_order(columns)
    copies = []
    for e, halo_ref in enumerate((before_ref, after_ref)):
        halo = []
        for part in range(2):
            flat = halo_ref[part].reshape(local * HALO, columns)
            halo.append(jnp.dot(flat, order, preferred_element_type=jnp.float32).astype(jnp.bfloat16))
        for a in range(local):
            windows = []
            for part in range(2):
                pieces = [halo[part][a * HALO : (a + 1) * HALO], edge_ref[e, part, a]]
                windows.append(jnp.concatenate(pieces if e == 0 else pieces[::-1], axis=0))
            both = filter_window(band_ref, a, windows)
            for core in range(CORES):
                for part in range(2):
                    start = part * BLOCK + core * CHUNK
                    done[e, core, part, a] = both[start : start + CHUNK]
        share = pl.ds(e * (out_ref.shape[0] - CORES), CORES)
        copies.append(pltpu.make_async_copy(done.at[e], out_ref.at[share], left.at[e]))
        copies[-1].start()
    for copy in copies:
        copy.wait()


def pair_kernel(pairs_ref, map_ref, got_ref, out_ref, got, image, phase, arrived):
    groups, _, slots = got.shape[:3]
    copies = [pltpu.make_async_copy(got_ref.at[g], got.at[g], arrived.at[g]) for g in range(groups)]
    for copy in copies:
        copy.start()
    for g in range(groups):
        copies[g].wait()
        for slot in range(slots):
            k = g * slots + slot
            real = got[g, 0, slot].astype(jnp.float32)
            imag = got[g, 1, slot].astype(jnp.float32)
            image[0, k] = real
            image[1, k] = imag
            image[2, k] = real + imag
            image[3, k] = real - imag
    lane = lax.broadcasted_iota(jnp.int32, (8, 128), 1)
    low = lane < 64

    def fold(value):
        upper, lower = value[:8], value[8:]
        return jnp.where(low, upper, lower) + pltpu.roll(jnp.where(low, lower, upper), 64, 1)

    def plus(total, term):
        return term if total is None else total + term

    def one_reference(i, carry):
        others = [pairs_ref[1, i * REACH + j] for j in range(REACH)]
        shared, first, second = [None] * REACH, [None] * REACH, [None] * REACH
        for look in range(LOOK):
            for side in range(2):
                where = (pl.ds(look * 16, 16), pl.ds(side * 128, 128))
                a_re, a_im, a_sum = (image[plane, i, where[0], where[1]] for plane in range(3))
                for j, k in enumerate(others):
                    b_re, b_sum, b_less = (image[plane, k, where[0], where[1]] for plane in (0, 2, 3))
                    shared[j] = plus(shared[j], b_re * a_sum)
                    first[j] = plus(first[j], a_im * b_less)
                    second[j] = plus(second[j], a_re * b_sum)
        for j in range(REACH):
            re, im = fold(shared[j] - first[j]), fold(shared[j] - second[j])
            least = float(LOOK**4)
            ratio = im * lax.rsqrt(jnp.maximum(re * re + im * im, least))
            phase[pl.ds(pl.multiple_of((i * REACH + j) * 8, 8), 8), :] = ratio
        return carry

    lax.fori_loop(0, groups * slots, one_reference, 0, unroll=8)

    table = map_ref[...]
    acqs, pairs = table.shape
    high = table.astype(jnp.bfloat16)
    rest = (table - high.astype(jnp.float32)).astype(jnp.bfloat16)
    stacked = jnp.concatenate([high, rest], axis=0)
    for t in range(8):
        value = phase[pl.ds(t, pairs, stride=8), :]
        v_high = value.astype(jnp.bfloat16)
        v_rest = (value - v_high.astype(jnp.float32)).astype(jnp.bfloat16)
        both = jnp.dot(stacked, v_high, preferred_element_type=jnp.float32)
        total = both[:acqs] + both[acqs:] + jnp.dot(high, v_rest, preferred_element_type=jnp.float32)
        out_ref[:, t * 128 : (t + 1) * 128] = total


def per_device(radar_stack, band_taps, pair_list):
    blocks_az = lax.axis_size("az")
    groups = lax.axis_size("acq")
    _, local, rows, columns = radar_stack.shape
    total_acq = groups * local
    up = [(i, i + 1) for i in range(blocks_az - 1)]
    down = [(j, i) for i, j in up]
    before = lax.ppermute(radar_stack[:, :, rows - HALO :], "az", up)
    after = lax.ppermute(radar_stack[:, :, :HALO], "az", down)
    taps = jnp.pad(band_taps.astype(jnp.float32), ((0, 0), (0, 0), (0, 2 * BLOCK - band_taps.shape[2])))
    pairs = pair_list.T
    bf16, f32 = jnp.bfloat16, jnp.float32

    def settings(mib):
        return dict(
            compiler_params=pltpu.CompilerParams(vmem_limit_bytes=mib * MIB),
            cost_estimate=pl.CostEstimate(flops=2_000_000_000, bytes_accessed=9_000_000, transcendentals=0),
        )

    def in_hbm(value):
        return pltpu.with_memory_space_constraint(value, pltpu.HBM)

    inner = groups - 2 * CORES
    filtered, band, edge, inverse_map = pl.pallas_call(
        interior_kernel,
        in_specs=[VMEM, VMEM, HBM],
        out_specs=[HBM, VMEM, VMEM, VMEM],
        out_shape=[
            pltpu.HBM((groups, 2, local, CHUNK, columns), bf16),
            pltpu.VMEM((local, 2, 2 * BLOCK, 2 * BLOCK), bf16),
            pltpu.VMEM((2, 2, local, REST, columns), bf16),
            jax.ShapeDtypeStruct((total_acq, pair_list.shape[0]), f32),
        ],
        scratch_shapes=[
            pltpu.VMEM(radar_stack.shape, bf16),
            pltpu.VMEM((2, rows, columns), bf16),
            pltpu.VMEM((local, inner, 2, CHUNK, columns), bf16),
            pltpu.SemaphoreType.DMA((local,)),
            pltpu.SemaphoreType.DMA((local,)),
        ],
        name="filter_interior",
        **settings(32),
    )(taps, pairs, in_hbm(radar_stack))
    filtered = pl.pallas_call(
        edge_kernel,
        in_specs=[VMEM] * 4 + [HBM],
        out_specs=HBM,
        out_shape=pltpu.HBM(filtered.shape, bf16),
        input_output_aliases={4: 0},
        scratch_shapes=[
            pltpu.VMEM((2, CORES, 2, local, CHUNK, columns), bf16),
            pltpu.SemaphoreType.DMA((2,)),
        ],
        name="filter_edges",
        **settings(24),
    )(band, edge, before, after, filtered)
    got = lax.all_to_all(filtered, "acq", 0, 0, tiled=True)
    return pl.pallas_call(
        pair_kernel,
        in_specs=[SMEM, VMEM, HBM],
        out_specs=VMEM,
        out_shape=jax.ShapeDtypeStruct((total_acq, CHUNK // LOOK * columns // LOOK), f32),
        scratch_shapes=[
            pltpu.VMEM((groups, 2, local, CHUNK, columns), bf16),
            pltpu.VMEM((4, total_acq, CHUNK, columns), f32),
            pltpu.VMEM((pair_list.shape[0] * 8, 128), f32),
            pltpu.SemaphoreType.DMA((groups,)),
        ],
        name="pairs_and_inversion",
        **settings(40),
    )(pairs, inverse_map, in_hbm(got))


def solution(mesh):
    return jax.shard_map(
        per_device,
        mesh=mesh,
        in_specs=(P(None, "acq", "az", None), P(None, "acq", None), P()),
        out_specs=P(None, ("az", "acq")),
        check_vma=False,
    )
```

time: 106 us -> 87.3 us (0.82)
  the two profiles are of different devices: /device:TPU:123 before, /device:TPU:4 now
where the time goes in v2:
time: 87.3 us; the launch traced here: 87 us
  blocking collectives  56.4 us (65%)
  Pallas kernels  19 us (22%)
  starting transfers between devices  7.81 us (9%)
  local copies, waits for them, and re-layouts  1.75 us (2%)
  waiting for transfers between devices  1.29 us (1%)
    all_to_all x1, blocking collectives, per_device(): got = lax.all_to_all(filtered, 'acq', 0, 0, tiled=True)  56.4 us
    pallas_call x1, Pallas kernels, per_device(): pl.pallas_call(interior_kernel, in_specs=[VMEM, VMEM, HBM], out_specs=[HB...  8.67 us
    pallas_call x1, Pallas kernels, per_device(): pl.pallas_call(pair_kernel, in_specs=[SMEM, VMEM, HBM], out_specs=VMEM, o...  8.42 us
    ppermute x1, starting transfers between devices, per_device(): after = lax.ppermute(radar_stack[:, :, :HALO], 'az', down)  5.89 us
    ppermute x1, starting transfers between devices, per_device(): before = lax.ppermute(radar_stack[:, :, rows - HALO:], 'az', up)  1.92 us
    pallas_call x1, Pallas kernels, per_device(): pl.pallas_call(edge_kernel, in_specs=[VMEM] * 4 + [HBM], out_specs=HBM, o...  1.87 us
  transfers between devices with their start and end apart: 2, of which 1 were waited for; matrix products, arithmetic and copies ran while one was open for 1% of the time, Pallas kernels for 10%

profile of v2, /device:TPU:4, one launch (start us, length us, event | category | flops | bytes accessed | tf_op | source)
XLA Modules:
  0.0 87.0 jit_solution(11958097263999267674)
XLA Ops:
  0.0 1.1 %fusion = (bf16[2,4,64,256]{3,2,1,0:T(8,128)(2,1)S(1)}, bf16[2,4,64,256]{3,2,1,0:T(8,128)(2,1)S(1)}) fusion(bf16[2,4,1024,256]{3,2,1,0:T(8,128)(2,1)} %image_ref.1), kind=kLoop, calls=%fused_computation.1 | loop fusion | bytes 1048576 | tf_op jit(solution)/shard_map/slice | solution.py:212
  1.1 5.9 %collective-permute-start.1 = (bf16[2,4,64,256]{3,2,1,0:T(8,128)(2,1)S(1)}, bf16[2,4,64,256]{3,2,1,0:T(8,128)(2,1)S(1)}, u32[]{:S(2)}, u32[]{:S(2)}) collective-permute-start(bf16[2,4,64,256]{3,2,1,0:T(8,128)(2,1)S(1)} %get-tuple-element.13), channel_id=1, source_target_pairs={{16,0},{32,16},{48,32},{64,48},{80,64},{96,80},{112,96},{17,1},{33... | collective-permute-start | bytes 786440 | tf_op jit(solution)/shard_map/ppermute | solution.py:212
  7.0 1.9 %collective-permute-start = (bf16[2,4,64,256]{3,2,1,0:T(8,128)(2,1)S(1)}, bf16[2,4,64,256]{3,2,1,0:T(8,128)(2,1)S(1)}, u32[]{:S(2)}, u32[]{:S(2)}) collective-permute-start(bf16[2,4,64,256]{3,2,1,0:T(8,128)(2,1)S(1)} %get-tuple-element.14), channel_id=1, source_target_pairs={{0,16},{16,32},{32,48},{48,64},{64,80},{80,96},{96,112},{1,17},{17... | collective-permute-start | bytes 786440 | tf_op jit(solution)/shard_map/ppermute | solution.py:211
  8.9 0.7 pad_convert_fusion.taps_ref
  9.6 0.0 copy-start
  9.6 0.7 copy-done
  10.3 8.7 %filter_interior.1 = (bf16[16,2,4,64,256]{4,3,2,1,0:T(8,128)(2,1)}, bf16[4,2,256,256]{3,2,1,0:T(8,128)(2,1)S(1)}, bf16[2,2,4,192,256]{4,3,2,1,0:T(8,128)(2,1)S(1)}, f32[64,256]{1,0:T(8,128)S(1)}) custom-call(f32[2,4,256]{2,1,0:T(4,128)S(1)} %pad_convert_fusion.taps_ref, s32[2,256]{1,0:T(2,128)S(1)} %bitcast.1, bf16[2,4,1024,256]{3,2,1,0:T(8,128)(2,1)} %image_ref.1), custom_call_target="tpu_custom_call" | custom-call | flops 2000000000 | bytes 9000000 | tf_op jit(solution)/shard_map/filter_interior/pallas_call | solution.py:227
  18.9 0.0 collective-permute-done.1.after_ref
  19.0 1.3 %collective-permute-done.before_ref = bf16[2,4,64,256]{3,2,1,0:T(8,128)(2,1)S(1)} collective-permute-done((bf16[2,4,64,256]{3,2,1,0:T(8,128)(2,1)S(1)}, bf16[2,4,64,256]{3,2,1,0:T(8,128)(2,1)S(1)}, u32[]{:S(2)}, u32[]{:S(2)}) %collective-permute-start) | collective-permute-done | bytes 262176 | tf_op jit(solution)/shard_map/ppermute | solution.py:211
  20.2 1.9 %filter_edges.1 = bf16[16,2,4,64,256]{4,3,2,1,0:T(8,128)(2,1)} custom-call(bf16[4,2,256,256]{3,2,1,0:T(8,128)(2,1)S(1)} %get-tuple-element.10.band_ref, bf16[2,2,4,192,256]{4,3,2,1,0:T(8,128)(2,1)S(1)} %get-tuple-element.11.edge_ref, bf16[2,4,64,256]{3,2,1,0:T(8,128)(2,1)S(1)} %collective-permute-done.before_ref, ...), custom_call_target="tpu_custom_call", output_to_operand_aliasing={{}: (4, {})} | custom-call | flops 2000000000 | bytes 9000000 | tf_op jit(solution)/shard_map/filter_edges/pallas_call | solution.py:247
  22.1 0.0 copy-start.1
  22.1 56.4 %all_to_all.5.got_ref = bf16[16,2,4,64,256]{4,3,2,1,0:T(8,128)(2,1)} all-to-all(bf16[16,2,4,64,256]{4,3,2,1,0:T(8,128)(2,1)} %filter_edges.1), channel_id=1, replica_groups=mesh['az'=8,'acq'=16] {'acq'}, dimensions={0} | all-to-all | bytes 8388608 | tf_op jit(solution)/shard_map/all_to_all | solution.py:260
  78.5 0.0 copy-done.1
  78.5 8.4 %pairs_and_inversion.1 = f32[64,1024]{1,0:T(8,128)} custom-call(s32[2,256]{1,0:T(2,128)S(1)} %bitcast.2, f32[64,256]{1,0:T(8,128)S(1)} %get-tuple-element.9.map_ref, bf16[16,2,4,64,256]{4,3,2,1,0:T(8,128)(2,1)} %all_to_all.5.got_ref), custom_call_target="tpu_custom_call" | custom-call | flops 2000000000 | bytes 9000000 | tf_op jit(solution)/shard_map/pairs_and_inversion/pallas_call | solution.py:261
Async XLA Ops:
  1.1 17.9 %collective-permute-start.1 = (bf16[2,4,64,256]{3,2,1,0:T(8,128)(2,1)S(1)}, bf16[2,4,64,256]{3,2,1,0:T(8,128)(2,1)S(1)}, u32[]{:S(2)}, u32[]{:S(2)}) collective-permute-start(bf16[2,4,64,256]{3,2,1,0:T(8,128)(2,1)S(1)} %get-tuple-element.13), channel_id=1, source_target_pairs={{16,0},{32,16},{48,32},{64,48},{80,64},{96,80},{112,96},{17,1},{33... | collective-permute-start | bytes 786440 | tf_op jit(solution)/shard_map/ppermute | solution.py:212
  7.0 13.3 %collective-permute-start = (bf16[2,4,64,256]{3,2,1,0:T(8,128)(2,1)S(1)}, bf16[2,4,64,256]{3,2,1,0:T(8,128)(2,1)S(1)}, u32[]{:S(2)}, u32[]{:S(2)}) collective-permute-start(bf16[2,4,64,256]{3,2,1,0:T(8,128)(2,1)S(1)} %get-tuple-element.14), channel_id=1, source_target_pairs={{0,16},{16,32},{32,48},{48,64},{64,80},{80,96},{96,112},{1,17},{17... | collective-permute-start | bytes 786440 | tf_op jit(solution)/shard_map/ppermute | solution.py:211
  9.6 0.7 copy-start
  22.1 56.4 %copy-start.1 = (s32[256,2]{0,1:T(2,128)S(1)}, s32[256,2]{0,1:T(2,128)}, u32[]{:S(2)}) copy-start(s32[256,2]{0,1:T(2,128)} %param.5) | copy-start | bytes 6148

commit v3 on v2

--- a/solution.py
+++ b/solution.py
@@ -12,7 +12,7 @@
 HALO = 64
 REST = 2 * BLOCK - HALO
 CORES = 2
-SOLVER_STEPS = 3
+SOLVER_STEPS = 2
 RIDGE = 1.0
 MIB = 1 << 20
 VMEM = pl.BlockSpec(memory_space=pltpu.VMEM)
@@ -53,10 +53,10 @@
     return group // (CHIPS * CORES), group // CORES % CHIPS, group % CORES
 
 
-def elimination(pairs_ref, map_ref):
+def elimination(pairs, map_ref):
     total = map_ref.shape[0]
     label = lax.broadcasted_iota(jnp.int32, map_ref.shape, 0)
-    incidence = jnp.where(label == pairs_ref[1:2, :], 1.0, 0.0) - jnp.where(label == pairs_ref[0:1, :], 1.0, 0.0)
+    incidence = jnp.where(label == pairs[1:2, :], 1.0, 0.0) - jnp.where(label == pairs[0:1, :], 1.0, 0.0)
     exact = incidence.astype(jnp.bfloat16)
     normal = lax.dot_general(exact, exact, (((1,), (1,)), ((), ())), preferred_element_type=jnp.float32)
     row = lax.broadcasted_iota(jnp.int32, (total, total), 0)
@@ -80,22 +80,34 @@
 
 
 def interior_kernel(
-    taps_ref, pairs_ref, image_ref, out_ref, band_ref, edge_ref, map_ref, image, ordered, done, arrived, left
+    taps_ref, pairs_ref, image_ref, out_ref, band_ref, edge_ref, map_ref, pairs, image, ordered, done, arrived, left
 ):
     _, local, rows, columns = image.shape
     blocks = rows // BLOCK
     inward = [pltpu.make_async_copy(image_ref.at[:, a], image.at[:, a], arrived.at[a]) for a in range(local)]
     inner = pl.ds(CORES, CORES * (blocks - 2))
     outward = [pltpu.make_async_copy(done.at[a], out_ref.at[inner, :, a], left.at[a]) for a in range(local)]
+    listed = pltpu.make_async_copy(pairs_ref, pairs, arrived.at[local])
+    listed.start()
     for copy in inward:
         copy.start()
     order = column_order(columns)
-    solver = elimination(pairs_ref, map_ref)
+    fill_bands(taps_ref, band_ref.at[0], 0)
+    listed.wait()
+    solver = elimination(pairs[...], map_ref)
+
+    def solve(steps):
+        for _ in range(steps):
+            next(solver, None)
+
+    for a in range(1, local):
+        fill_bands(taps_ref, band_ref.at[a], a)
+        solve(SOLVER_STEPS)
     for a in range(local):
-        fill_bands(taps_ref, band_ref.at[a], a)
         inward[a].wait()
         for part in range(2):
             ordered[part] = jnp.dot(image[part, a], order, preferred_element_type=jnp.float32).astype(jnp.bfloat16)
+            solve(SOLVER_STEPS)
             edge_ref[0, part, a] = ordered[part, :REST, :]
             edge_ref[1, part, a] = ordered[part, rows - REST :, :]
         for block in range(1, blocks - 1):
@@ -105,25 +117,24 @@
                 for part in range(2):
                     start = part * BLOCK + core * CHUNK
                     done[a, (block - 1) * CORES + core, part] = both[start : start + CHUNK]
-            for _ in range(SOLVER_STEPS):
-                next(solver, None)
+            solve(SOLVER_STEPS)
         outward[a].start()
-    for _ in solver:
-        pass
+    solve(1 + 8 * REST)
     for copy in outward:
         copy.wait()
 
 
-def edge_kernel(band_ref, edge_ref, before_ref, after_ref, filled_ref, out_ref, done, left):
+def edge_kernel(odd_ref, band_ref, edge_ref, even_ref, odd_pairs_ref, filled_ref, out_ref, done, left):
     del filled_ref
-    local, columns = before_ref.shape[1], before_ref.shape[3]
+    local, columns = even_ref.shape[1], even_ref.shape[3]
     order = column_order(columns)
     copies = []
-    for e, halo_ref in enumerate((before_ref, after_ref)):
-        halo = []
-        for part in range(2):
-            flat = halo_ref[part].reshape(local * HALO, columns)
-            halo.append(jnp.dot(flat, order, preferred_element_type=jnp.float32).astype(jnp.bfloat16))
+    received = []
+    for halo_ref in (even_ref, odd_pairs_ref):
+        flat = (halo_ref[part].reshape(local * HALO, columns) for part in range(2))
+        received.append([jnp.dot(f, order, preferred_element_type=jnp.float32).astype(jnp.bfloat16) for f in flat])
+    for e in range(2):
+        halo = [jnp.where(odd_ref[0] == 1 - e, one, two) for one, two in zip(*received)]
         for a in range(local):
             windows = []
             for part in range(2):
@@ -141,21 +152,17 @@
         copy.wait()
 
 
-def pair_kernel(pairs_ref, map_ref, got_ref, out_ref, got, image, phase, arrived):
+def pair_kernel(pairs_ref, map_ref, got, out_ref, image, phase):
     groups, _, slots = got.shape[:3]
-    copies = [pltpu.make_async_copy(got_ref.at[g], got.at[g], arrived.at[g]) for g in range(groups)]
-    for copy in copies:
-        copy.start()
-    for g in range(groups):
-        copies[g].wait()
-        for slot in range(slots):
-            k = g * slots + slot
-            real = got[g, 0, slot].astype(jnp.float32)
-            imag = got[g, 1, slot].astype(jnp.float32)
-            image[0, k] = real
-            image[1, k] = imag
-            image[2, k] = real + imag
-            image[3, k] = real - imag
+
+    def widen(g, slot):
+        k = g * slots + slot
+        real = got[g, 0, slot].astype(jnp.float32)
+        imag = got[g, 1, slot].astype(jnp.float32)
+        image[0, k] = real
+        image[1, k] = imag
+        image[2, k] = real - imag
+
     lane = lax.broadcasted_iota(jnp.int32, (8, 128), 1)
     low = lane < 64
 
@@ -166,26 +173,30 @@
     def plus(total, term):
         return term if total is None else total + term
 
-    def one_reference(i, carry):
+    def one_reference(i):
         others = [pairs_ref[1, i * REACH + j] for j in range(REACH)]
-        shared, first, second = [None] * REACH, [None] * REACH, [None] * REACH
+        reals, imags, crossed = [None] * REACH, [None] * REACH, [None] * REACH
         for look in range(LOOK):
             for side in range(2):
                 where = (pl.ds(look * 16, 16), pl.ds(side * 128, 128))
-                a_re, a_im, a_sum = (image[plane, i, where[0], where[1]] for plane in range(3))
+                a_re, a_im = (image[plane, i, where[0], where[1]] for plane in range(2))
+                a_sum = a_re + a_im
                 for j, k in enumerate(others):
-                    b_re, b_sum, b_less = (image[plane, k, where[0], where[1]] for plane in (0, 2, 3))
-                    shared[j] = plus(shared[j], b_re * a_sum)
-                    first[j] = plus(first[j], a_im * b_less)
-                    second[j] = plus(second[j], a_re * b_sum)
+                    b_re, b_im, b_less = (image[plane, k, where[0], where[1]] for plane in range(3))
+                    reals[j] = plus(reals[j], a_re * b_re)
+                    imags[j] = plus(imags[j], a_im * b_im)
+                    crossed[j] = plus(crossed[j], a_sum * b_less)
         for j in range(REACH):
-            re, im = fold(shared[j] - first[j]), fold(shared[j] - second[j])
+            re = fold(reals[j] + imags[j])
+            im = fold(crossed[j] - reals[j] + imags[j])
             least = float(LOOK**4)
             ratio = im * lax.rsqrt(jnp.maximum(re * re + im * im, least))
             phase[pl.ds(pl.multiple_of((i * REACH + j) * 8, 8), 8), :] = ratio
-        return carry
-
-    lax.fori_loop(0, groups * slots, one_reference, 0, unroll=8)
+
+    for g in range(groups):
+        for slot in range(slots):
+            widen(g, slot)
+    lax.fori_loop(0, groups * slots, lambda i, carry: one_reference(i), None, unroll=8)
 
     table = map_ref[...]
     acqs, pairs = table.shape
@@ -206,10 +217,13 @@
     groups = lax.axis_size("acq")
     _, local, rows, columns = radar_stack.shape
     total_acq = groups * local
-    up = [(i, i + 1) for i in range(blocks_az - 1)]
-    down = [(j, i) for i, j in up]
-    before = lax.ppermute(radar_stack[:, :, rows - HALO :], "az", up)
-    after = lax.ppermute(radar_stack[:, :, :HALO], "az", down)
+    odd = lax.axis_index("az") % 2
+    first, final = radar_stack[:, :, :HALO], radar_stack[:, :, rows - HALO :]
+    meet = [[(i, i + 1) for i in range(start, blocks_az - 1, 2)] for start in range(2)]
+    even_pairs, odd_pairs = (
+        lax.ppermute(jnp.where(odd == start, final, first), "az", ones + [(j, i) for i, j in ones])
+        for start, ones in enumerate(meet)
+    )
     taps = jnp.pad(band_taps.astype(jnp.float32), ((0, 0), (0, 0), (0, 2 * BLOCK - band_taps.shape[2])))
     pairs = pair_list.T
     bf16, f32 = jnp.bfloat16, jnp.float32
@@ -226,7 +240,7 @@
     inner = groups - 2 * CORES
     filtered, band, edge, inverse_map = pl.pallas_call(
         interior_kernel,
-        in_specs=[VMEM, VMEM, HBM],
+        in_specs=[VMEM, HBM, HBM],
         out_specs=[HBM, VMEM, VMEM, VMEM],
         out_shape=[
             pltpu.HBM((groups, 2, local, CHUNK, columns), bf16),
@@ -235,43 +249,42 @@
             jax.ShapeDtypeStruct((total_acq, pair_list.shape[0]), f32),
         ],
         scratch_shapes=[
+            pltpu.VMEM(pairs.shape, pairs.dtype),
             pltpu.VMEM(radar_stack.shape, bf16),
             pltpu.VMEM((2, rows, columns), bf16),
             pltpu.VMEM((local, inner, 2, CHUNK, columns), bf16),
-            pltpu.SemaphoreType.DMA((local,)),
+            pltpu.SemaphoreType.DMA((local + 1,)),
             pltpu.SemaphoreType.DMA((local,)),
         ],
         name="filter_interior",
         **settings(32),
-    )(taps, pairs, in_hbm(radar_stack))
+    )(taps, in_hbm(pairs), in_hbm(radar_stack))
     filtered = pl.pallas_call(
         edge_kernel,
-        in_specs=[VMEM] * 4 + [HBM],
+        in_specs=[SMEM] + [VMEM] * 4 + [HBM],
         out_specs=HBM,
         out_shape=pltpu.HBM(filtered.shape, bf16),
-        input_output_aliases={4: 0},
+        input_output_aliases={5: 0},
         scratch_shapes=[
             pltpu.VMEM((2, CORES, 2, local, CHUNK, columns), bf16),
             pltpu.SemaphoreType.DMA((2,)),
         ],
         name="filter_edges",
         **settings(24),
-    )(band, edge, before, after, filtered)
+    )(odd.reshape(1), band, edge, even_pairs, odd_pairs, filtered)
     got = lax.all_to_all(filtered, "acq", 0, 0, tiled=True)
     return pl.pallas_call(
         pair_kernel,
-        in_specs=[SMEM, VMEM, HBM],
+        in_specs=[SMEM, VMEM, VMEM],
         out_specs=VMEM,
         out_shape=jax.ShapeDtypeStruct((total_acq, CHUNK // LOOK * columns // LOOK), f32),
         scratch_shapes=[
-            pltpu.VMEM((groups, 2, local, CHUNK, columns), bf16),
-            pltpu.VMEM((4, total_acq, CHUNK, columns), f32),
+            pltpu.VMEM((3, total_acq, CHUNK, columns), f32),
             pltpu.VMEM((pair_list.shape[0] * 8, 128), f32),
-            pltpu.SemaphoreType.DMA((groups,)),
         ],
         name="pairs_and_inversion",
-        **settings(40),
-    )(pairs, inverse_map, in_hbm(got))
+        **settings(24),
+    )(pairs, inverse_map, pltpu.with_memory_space_constraint(got, pltpu.VMEM))
 
 
 def solution(mesh):

time: 87.3 us -> 80.8 us (0.926)
  Pallas kernels: 19 us -> 16.3 us
  starting transfers between devices: 7.81 us -> 5.97 us
  local copies, waits for them, and re-layouts: 1.75 us -> 0.01 us
  waiting for transfers between devices: 1.29 us -> 0.01 us
  other arithmetic: 0.69 us -> 1.76 us
    pallas_call x3, Pallas kernels: 19 us -> 16.3 us  [the longest x1 7.73 us: per_device(): pl.pallas_call(interior_kernel, in_specs=[VMEM, HBM, HBM], out_specs=[HBM...]
    ppermute x2, starting transfers between devices: 7.81 us -> 5.97 us  [per_device(): lax.ppermute(jnp.where(odd == start, final, first), 'az', ones + [(j, i)...]
    ppermute x2, waiting for transfers between devices: 1.29 us -> 0.01 us  [per_device(): lax.ppermute(jnp.where(odd == start, final, first), 'az', ones + [(j, i)...]
    select_n x0 -> x1, other arithmetic: none -> 1.07 us  [per_device(): jnp.where(odd == start, final, first)]
    slice x1 -> x0, local copies, waits for them, and re-layouts: 1.06 us -> none  [per_device(): after = lax.ppermute(radar_stack[:, :, :HALO], 'az', down)]
  transfers between devices with their start and end apart: 2 -> 2, of which waited for: 1 -> 0; matrix products, arithmetic and copies ran while one was open for 1% -> 1% of each run, Pallas kernels for 10% -> 10%
where the time goes in v3:
time: 80.8 us; the launch traced here: 80.4 us
  blocking collectives  56.3 us (70%)
  Pallas kernels  16.3 us (20%)
  starting transfers between devices  5.97 us (7%)
  other arithmetic  1.76 us (2%)
    all_to_all x1, blocking collectives, per_device(): got = lax.all_to_all(filtered, 'acq', 0, 0, tiled=True)  56.3 us
    pallas_call x1, Pallas kernels, per_device(): pl.pallas_call(interior_kernel, in_specs=[VMEM, HBM, HBM], out_specs=[HBM...  7.73 us
    pallas_call x1, Pallas kernels, per_device(): pl.pallas_call(pair_kernel, in_specs=[SMEM, VMEM, VMEM], out_specs=VMEM,...  6.81 us
    ppermute x2, starting transfers between devices, per_device(): lax.ppermute(jnp.where(odd == start, final, first), 'az', ones + [(j, i)...  5.97 us
    pallas_call x1, Pallas kernels, per_device(): pl.pallas_call(edge_kernel, in_specs=[SMEM] + [VMEM] * 4 + [HBM], out_spe...  1.79 us
  transfers between devices with their start and end apart: 2, of which 0 were waited for; matrix products, arithmetic and copies ran while one was open for 1% of the time, Pallas kernels for 10%

profile of v3, /device:TPU:4, one launch (start us, length us, event | category | flops | bytes accessed | tf_op | source)
XLA Modules:
  0.0 80.4 jit_solution(14830669446201850171)
XLA Ops:
  0.0 1.1 %broadcast_select_fusion = (bf16[2,4,64,256]{3,2,1,0:T(8,128)(2,1)S(1)}, bf16[2,4,64,256]{3,2,1,0:T(8,128)(2,1)S(1)}) fusion(pred[]{:T(512)S(6)} %eq.9, bf16[2,4,1024,256]{3,2,1,0:T(8,128)(2,1)} %image_ref.1, pred[]{:T(512)S(6)} %eq.8), kind=kLoop, calls=%fused_computation | loop fusion | flops 262144 | bytes 1048578 | tf_op jit(solution)/shard_map/jit(_where)/select_n | solution.py:224
  1.1 5.9 %collective-permute-start.1 = (bf16[2,4,64,256]{3,2,1,0:T(8,128)(2,1)S(1)}, bf16[2,4,64,256]{3,2,1,0:T(8,128)(2,1)S(1)}, u32[]{:S(2)}, u32[]{:S(2)}) collective-permute-start(bf16[2,4,64,256]{3,2,1,0:T(8,128)(2,1)S(1)} %get-tuple-element.13), channel_id=1, source_target_pairs={{16,32},{48,64},{80,96},{32,16},{64,48},{96,80},{17,33},{49,65},{8... | collective-permute-start | bytes 786440 | tf_op jit(solution)/shard_map/ppermute | solution.py:224
  7.0 0.1 collective-permute-start
  7.1 0.7 pad_convert_fusion.taps_ref
  7.8 7.7 %filter_interior.1 = (bf16[16,2,4,64,256]{4,3,2,1,0:T(8,128)(2,1)}, bf16[4,2,256,256]{3,2,1,0:T(8,128)(2,1)S(1)}, bf16[2,2,4,192,256]{4,3,2,1,0:T(8,128)(2,1)S(1)}, f32[64,256]{1,0:T(8,128)S(1)}) custom-call(f32[2,4,256]{2,1,0:T(4,128)S(1)} %pad_convert_fusion.taps_ref, s32[2,256]{1,0:T(2,128)} %bitcast.2, bf16[2,4,1024,256]{3,2,1,0:T(8,128)(2,1)} %image_ref.1), custom_call_target="tpu_custom_call" | custom-call | flops 2000000000 | bytes 9000000 | tf_op jit(solution)/shard_map/filter_interior/pallas_call | solution.py:241
  15.5 0.0 collective-permute-done.1.odd_pairs_ref
  15.5 0.0 collective-permute-done.even_ref
  15.5 1.8 %filter_edges.1 = bf16[16,2,4,64,256]{4,3,2,1,0:T(8,128)(2,1)} custom-call(s32[1]{0:T(128)} %bitcast.1.odd_ref, bf16[4,2,256,256]{3,2,1,0:T(8,128)(2,1)S(1)} %get-tuple-element.10.band_ref, bf16[2,2,4,192,256]{4,3,2,1,0:T(8,128)(2,1)S(1)} %get-tuple-element.11.edge_ref, ...), custom_call_target="tpu_custom_call", output_to_operand_aliasing={{}: (5, {})} | custom-call | flops 2000000000 | bytes 9000000 | tf_op jit(solution)/shard_map/filter_edges/pallas_call | solution.py:262
  17.3 0.0 copy-start
  17.3 56.3 %all_to_all.5.got = bf16[16,2,4,64,256]{4,3,2,1,0:T(8,128)(2,1)S(1)} all-to-all(bf16[16,2,4,64,256]{4,3,2,1,0:T(8,128)(2,1)} %filter_edges.1), channel_id=1, replica_groups=mesh['az'=8,'acq'=16] {'acq'}, dimensions={0} | all-to-all | bytes 8388608 | tf_op jit(solution)/shard_map/all_to_all | solution.py:275
  73.6 0.0 copy-done
  73.6 6.8 %pairs_and_inversion.1 = f32[64,1024]{1,0:T(8,128)} custom-call(s32[2,256]{1,0:T(2,128)S(1)} %bitcast.3, f32[64,256]{1,0:T(8,128)S(1)} %get-tuple-element.9.map_ref, bf16[16,2,4,64,256]{4,3,2,1,0:T(8,128)(2,1)S(1)} %all_to_all.5.got), custom_call_target="tpu_custom_call" | custom-call | flops 2000000000 | bytes 9000000 | tf_op jit(solution)/shard_map/pairs_and_inversion/pallas_call | solution.py:276
Async XLA Ops:
  1.1 14.4 %collective-permute-start.1 = (bf16[2,4,64,256]{3,2,1,0:T(8,128)(2,1)S(1)}, bf16[2,4,64,256]{3,2,1,0:T(8,128)(2,1)S(1)}, u32[]{:S(2)}, u32[]{:S(2)}) collective-permute-start(bf16[2,4,64,256]{3,2,1,0:T(8,128)(2,1)S(1)} %get-tuple-element.13), channel_id=1, source_target_pairs={{16,32},{48,64},{80,96},{32,16},{64,48},{96,80},{17,33},{49,65},{8... | collective-permute-start | bytes 786440 | tf_op jit(solution)/shard_map/ppermute | solution.py:224
  7.0 8.5 %collective-permute-start = (bf16[2,4,64,256]{3,2,1,0:T(8,128)(2,1)S(1)}, bf16[2,4,64,256]{3,2,1,0:T(8,128)(2,1)S(1)}, u32[]{:S(2)}, u32[]{:S(2)}) collective-permute-start(bf16[2,4,64,256]{3,2,1,0:T(8,128)(2,1)S(1)} %get-tuple-element.14), channel_id=1, source_target_pairs={{0,16},{32,48},{64,80},{96,112},{16,0},{48,32},{80,64},{112,96},{1... | collective-permute-start | bytes 786440 | tf_op jit(solution)/shard_map/ppermute | solution.py:224
  17.3 56.3 %copy-start = (s32[256,2]{0,1:T(2,128)S(1)}, s32[256,2]{0,1:T(2,128)}, u32[]{:S(2)}) copy-start(s32[256,2]{0,1:T(2,128)} %param.5) | copy-start | bytes 6148

commit v4 on v3

--- a/solution.py
+++ b/solution.py
@@ -12,6 +12,7 @@
 HALO = 64
 REST = 2 * BLOCK - HALO
 CORES = 2
+AHEAD = 2
 SOLVER_STEPS = 2
 RIDGE = 1.0
 MIB = 1 << 20
@@ -64,9 +65,22 @@
     unit = jnp.where(row == column, 1.0, 0.0)
     table = jnp.concatenate([normal + RIDGE * unit, unit], axis=1)
     index = lax.broadcasted_iota(jnp.int32, table.shape, 0)
+    def spread(k):
+        return jnp.broadcast_to(table[:, k : k + 1], table.shape)
+
+    spreads = [spread(k) for k in range(AHEAD)]
     for k in range(total):
-        scaled = table[k : k + 1, :] * (1.0 / table[k : k + 1, k : k + 1])
-        table = jnp.where(index == k, scaled, table - table[:, k : k + 1] * scaled)
+        if k + AHEAD < total:
+            spreads.append(spread(k + AHEAD))
+        pivot = spreads.pop(0)
+        scale = 1.0 / pivot[k : k + 1, :]
+
+        def step(value):
+            scaled = value[k : k + 1, :] * scale
+            return jnp.where(index == k, scaled, value - pivot * scaled)
+
+        table = step(table)
+        spreads = [step(value) for value in spreads]
         yield
     map_ref[...] = jnp.dot(
         table[:, total:], incidence, precision=lax.Precision.HIGHEST, preferred_element_type=jnp.float32
@@ -218,10 +232,13 @@
     _, local, rows, columns = radar_stack.shape
     total_acq = groups * local
     odd = lax.axis_index("az") % 2
-    first, final = radar_stack[:, :, :HALO], radar_stack[:, :, rows - HALO :]
     meet = [[(i, i + 1) for i in range(start, blocks_az - 1, 2)] for start in range(2)]
     even_pairs, odd_pairs = (
-        lax.ppermute(jnp.where(odd == start, final, first), "az", ones + [(j, i) for i, j in ones])
+        lax.ppermute(
+            lax.dynamic_slice_in_dim(radar_stack, jnp.where(odd == start, rows - HALO, 0), HALO, 2),
+            "az",
+            ones + [(j, i) for i, j in ones],
+        )
         for start, ones in enumerate(meet)
     )
     taps = jnp.pad(band_taps.astype(jnp.float32), ((0, 0), (0, 0), (0, 2 * BLOCK - band_taps.shape[2])))

time: 80.8 us -> 80 us (0.990)
  Pallas kernels: 16.3 us -> 14.4 us
  waiting for transfers between devices: 0.01 us -> 1.22 us
  other arithmetic: 1.76 us -> 0.69 us
  local copies, waits for them, and re-layouts: 0.01 us -> 1.08 us
    pallas_call x1, Pallas kernels: 7.73 us -> 5.84 us  [per_device(): pl.pallas_call(interior_kernel, in_specs=[VMEM, HBM, HBM], out_specs=[HBM...]
    ppermute x2, waiting for transfers between devices: 0.01 us -> 1.22 us  [per_device(): lax.ppermute(lax.dynamic_slice_in_dim(radar_stack, jnp.where(odd == start...]
    dynamic_slice x0 -> x1, local copies, waits for them, and re-layouts: none -> 1.07 us  [per_device(): lax.dynamic_slice_in_dim(radar_stack, jnp.where(odd == start, rows - HALO...]
    select_n x1 -> x0, other arithmetic: 1.07 us -> none  [per_device(): jnp.where(odd == start, final, first)]
  transfers between devices with their start and end apart: 2 -> 2, of which waited for: 0 -> 2; matrix products, arithmetic and copies ran while one was open for 1% -> 1% of each run, Pallas kernels for 10% -> 7%
where the time goes in v4:
time: 80 us; the launch traced here: 79.7 us
  blocking collectives  56.3 us (70%)
  Pallas kernels  14.4 us (18%)
  starting transfers between devices  5.97 us (7%)
  waiting for transfers between devices  1.22 us (2%)
  local copies, waits for them, and re-layouts  1.08 us (1%)
    all_to_all x1, blocking collectives, per_device(): got = lax.all_to_all(filtered, 'acq', 0, 0, tiled=True)  56.3 us
    pallas_call x1, Pallas kernels, per_device(): pl.pallas_call(pair_kernel, in_specs=[SMEM, VMEM, VMEM], out_specs=VMEM,...  6.8 us
    ppermute x2, starting transfers between devices, per_device(): lax.ppermute(lax.dynamic_slice_in_dim(radar_stack, jnp.where(odd == start...  5.97 us
    pallas_call x1, Pallas kernels, per_device(): pl.pallas_call(interior_kernel, in_specs=[VMEM, HBM, HBM], out_specs=[HBM...  5.84 us
    pallas_call x1, Pallas kernels, per_device(): pl.pallas_call(edge_kernel, in_specs=[SMEM] + [VMEM] * 4 + [HBM], out_spe...  1.78 us
  transfers between devices with their start and end apart: 2, of which 2 were waited for; matrix products, arithmetic and copies ran while one was open for 1% of the time, Pallas kernels for 7%

profile of v4, /device:TPU:4, one launch (start us, length us, event | category | flops | bytes accessed | tf_op | source)
XLA Modules:
  0.0 79.7 jit_solution(13386224272161058149)
XLA Ops:
  0.0 1.1 %constant_dynamic-slice_fusion = (bf16[2,4,64,256]{3,2,1,0:T(8,128)(2,1)S(1)}, bf16[2,4,64,256]{3,2,1,0:T(8,128)(2,1)S(1)}) fusion(bf16[2,4,1024,256]{3,2,1,0:T(8,128)(2,1)} %image_ref.1, s32[]{:T(128)S(6)} %select_n.18, s32[]{:T(128)S(6)} %select_n.17), kind=kLoop, calls=%fused_computation.1 | loop fusion | bytes 1048584 | tf_op jit(solution)/shard_map/dynamic_slice | solution.py:238
  1.1 5.9 %collective-permute-start.1 = (bf16[2,4,64,256]{3,2,1,0:T(8,128)(2,1)S(1)}, bf16[2,4,64,256]{3,2,1,0:T(8,128)(2,1)S(1)}, u32[]{:S(2)}, u32[]{:S(2)}) collective-permute-start(bf16[2,4,64,256]{3,2,1,0:T(8,128)(2,1)S(1)} %get-tuple-element.13), channel_id=1, source_target_pairs={{16,32},{48,64},{80,96},{32,16},{64,48},{96,80},{17,33},{49,65},{8... | collective-permute-start | bytes 786440 | tf_op jit(solution)/shard_map/ppermute | solution.py:237
  7.0 0.1 collective-permute-start
  7.1 0.7 pad_convert_fusion.taps_ref
  7.8 5.8 %filter_interior.1 = (bf16[16,2,4,64,256]{4,3,2,1,0:T(8,128)(2,1)}, bf16[4,2,256,256]{3,2,1,0:T(8,128)(2,1)S(1)}, bf16[2,2,4,192,256]{4,3,2,1,0:T(8,128)(2,1)S(1)}, f32[64,256]{1,0:T(8,128)S(1)}) custom-call(f32[2,4,256]{2,1,0:T(4,128)S(1)} %pad_convert_fusion.taps_ref, s32[2,256]{1,0:T(2,128)} %bitcast.2, bf16[2,4,1024,256]{3,2,1,0:T(8,128)(2,1)} %image_ref.1), custom_call_target="tpu_custom_call" | custom-call | flops 2000000000 | bytes 9000000 | tf_op jit(solution)/shard_map/filter_interior/pallas_call | solution.py:258
  13.6 1.0 %collective-permute-done.1.odd_pairs_ref = bf16[2,4,64,256]{3,2,1,0:T(8,128)(2,1)S(1)} collective-permute-done((bf16[2,4,64,256]{3,2,1,0:T(8,128)(2,1)S(1)}, bf16[2,4,64,256]{3,2,1,0:T(8,128)(2,1)S(1)}, u32[]{:S(2)}, u32[]{:S(2)}) %collective-permute-start.1) | collective-permute-done | bytes 262176 | tf_op jit(solution)/shard_map/ppermute | solution.py:237
  14.6 0.2 collective-permute-done.even_ref
  14.8 1.8 %filter_edges.1 = bf16[16,2,4,64,256]{4,3,2,1,0:T(8,128)(2,1)} custom-call(s32[1]{0:T(128)} %bitcast.1.odd_ref, bf16[4,2,256,256]{3,2,1,0:T(8,128)(2,1)S(1)} %get-tuple-element.10.band_ref, bf16[2,2,4,192,256]{4,3,2,1,0:T(8,128)(2,1)S(1)} %get-tuple-element.11.edge_ref, ...), custom_call_target="tpu_custom_call", output_to_operand_aliasing={{}: (5, {})} | custom-call | flops 2000000000 | bytes 9000000 | tf_op jit(solution)/shard_map/filter_edges/pallas_call | solution.py:279
  16.6 0.0 copy-start
  16.6 56.3 %all_to_all.5.got = bf16[16,2,4,64,256]{4,3,2,1,0:T(8,128)(2,1)S(1)} all-to-all(bf16[16,2,4,64,256]{4,3,2,1,0:T(8,128)(2,1)} %filter_edges.1), channel_id=1, replica_groups=mesh['az'=8,'acq'=16] {'acq'}, dimensions={0} | all-to-all | bytes 8388608 | tf_op jit(solution)/shard_map/all_to_all | solution.py:292
  72.9 0.0 copy-done
  72.9 6.8 %pairs_and_inversion.1 = f32[64,1024]{1,0:T(8,128)} custom-call(s32[2,256]{1,0:T(2,128)S(1)} %bitcast.3, f32[64,256]{1,0:T(8,128)S(1)} %get-tuple-element.9.map_ref, bf16[16,2,4,64,256]{4,3,2,1,0:T(8,128)(2,1)S(1)} %all_to_all.5.got), custom_call_target="tpu_custom_call" | custom-call | flops 2000000000 | bytes 9000000 | tf_op jit(solution)/shard_map/pairs_and_inversion/pallas_call | solution.py:293
Async XLA Ops:
  1.1 13.6 %collective-permute-start.1 = (bf16[2,4,64,256]{3,2,1,0:T(8,128)(2,1)S(1)}, bf16[2,4,64,256]{3,2,1,0:T(8,128)(2,1)S(1)}, u32[]{:S(2)}, u32[]{:S(2)}) collective-permute-start(bf16[2,4,64,256]{3,2,1,0:T(8,128)(2,1)S(1)} %get-tuple-element.13), channel_id=1, source_target_pairs={{16,32},{48,64},{80,96},{32,16},{64,48},{96,80},{17,33},{49,65},{8... | collective-permute-start | bytes 786440 | tf_op jit(solution)/shard_map/ppermute | solution.py:237
  7.0 7.8 %collective-permute-start = (bf16[2,4,64,256]{3,2,1,0:T(8,128)(2,1)S(1)}, bf16[2,4,64,256]{3,2,1,0:T(8,128)(2,1)S(1)}, u32[]{:S(2)}, u32[]{:S(2)}) collective-permute-start(bf16[2,4,64,256]{3,2,1,0:T(8,128)(2,1)S(1)} %get-tuple-element.14), channel_id=1, source_target_pairs={{0,16},{32,48},{64,80},{96,112},{16,0},{48,32},{80,64},{112,96},{1... | collective-permute-start | bytes 786440 | tf_op jit(solution)/shard_map/ppermute | solution.py:237
  16.6 56.3 %copy-start = (s32[256,2]{0,1:T(2,128)S(1)}, s32[256,2]{0,1:T(2,128)}, u32[]{:S(2)}) copy-start(s32[256,2]{0,1:T(2,128)} %param.5) | copy-start | bytes 6148

commit v5 on v4

--- a/solution.py
+++ b/solution.py
@@ -158,10 +158,10 @@
             for core in range(CORES):
                 for part in range(2):
                     start = part * BLOCK + core * CHUNK
-                    done[e, core, part, a] = both[start : start + CHUNK]
-        share = pl.ds(e * (out_ref.shape[0] - CORES), CORES)
-        copies.append(pltpu.make_async_copy(done.at[e], out_ref.at[share], left.at[e]))
-        copies[-1].start()
+                    done[e, a, core, part] = both[start : start + CHUNK]
+            share = pl.ds(e * (out_ref.shape[0] - CORES), CORES)
+            copies.append(pltpu.make_async_copy(done.at[e, a], out_ref.at[share, :, a], left.at[e, a]))
+            copies[-1].start()
     for copy in copies:
         copy.wait()
 
@@ -210,7 +210,7 @@
     for g in range(groups):
         for slot in range(slots):
             widen(g, slot)
-    lax.fori_loop(0, groups * slots, lambda i, carry: one_reference(i), None, unroll=8)
+    lax.fori_loop(0, groups * slots, lambda i, carry: one_reference(i), None, unroll=16)
 
     table = map_ref[...]
     acqs, pairs = table.shape
@@ -283,8 +283,8 @@
         out_shape=pltpu.HBM(filtered.shape, bf16),
         input_output_aliases={5: 0},
         scratch_shapes=[
-            pltpu.VMEM((2, CORES, 2, local, CHUNK, columns), bf16),
-            pltpu.SemaphoreType.DMA((2,)),
+            pltpu.VMEM((2, local, CORES, 2, CHUNK, columns), bf16),
+            pltpu.SemaphoreType.DMA((2, local)),
         ],
         name="filter_edges",
         **settings(24),

time: 80 us -> 79.7 us (level)
  no operation moved by 1% of the time
where the time goes in v5:
time: 79.7 us; the launch traced here: 79.5 us
  blocking collectives  56.3 us (71%)
  Pallas kernels  14.2 us (18%)
  starting transfers between devices  5.97 us (7%)
  waiting for transfers between devices  1.22 us (2%)
  local copies, waits for them, and re-layouts  1.08 us (1%)
    all_to_all x1, blocking collectives, per_device(): got = lax.all_to_all(filtered, 'acq', 0, 0, tiled=True)  56.3 us
    pallas_call x1, Pallas kernels, per_device(): pl.pallas_call(pair_kernel, in_specs=[SMEM, VMEM, VMEM], out_specs=VMEM,...  6.58 us
    ppermute x2, starting transfers between devices, per_device(): lax.ppermute(lax.dynamic_slice_in_dim(radar_stack, jnp.where(odd == start...  5.97 us
    pallas_call x1, Pallas kernels, per_device(): pl.pallas_call(interior_kernel, in_specs=[VMEM, HBM, HBM], out_specs=[HBM...  5.84 us
    pallas_call x1, Pallas kernels, per_device(): pl.pallas_call(edge_kernel, in_specs=[SMEM] + [VMEM] * 4 + [HBM], out_spe...  1.75 us
  transfers between devices with their start and end apart: 2, of which 2 were waited for; matrix products, arithmetic and copies ran while one was open for 1% of the time, Pallas kernels for 7%

profile of v5, /device:TPU:4, one launch (start us, length us, event | category | flops | bytes accessed | tf_op | source)
XLA Modules:
  0.0 79.5 jit_solution(749192603195371123)
XLA Ops:
  0.0 1.1 %constant_dynamic-slice_fusion = (bf16[2,4,64,256]{3,2,1,0:T(8,128)(2,1)S(1)}, bf16[2,4,64,256]{3,2,1,0:T(8,128)(2,1)S(1)}) fusion(bf16[2,4,1024,256]{3,2,1,0:T(8,128)(2,1)} %image_ref.1, s32[]{:T(128)S(6)} %select_n.18, s32[]{:T(128)S(6)} %select_n.17), kind=kLoop, calls=%fused_computation.1 | loop fusion | bytes 1048584 | tf_op jit(solution)/shard_map/dynamic_slice | solution.py:238
  1.1 5.9 %collective-permute-start.1 = (bf16[2,4,64,256]{3,2,1,0:T(8,128)(2,1)S(1)}, bf16[2,4,64,256]{3,2,1,0:T(8,128)(2,1)S(1)}, u32[]{:S(2)}, u32[]{:S(2)}) collective-permute-start(bf16[2,4,64,256]{3,2,1,0:T(8,128)(2,1)S(1)} %get-tuple-element.13), channel_id=1, source_target_pairs={{16,32},{48,64},{80,96},{32,16},{64,48},{96,80},{17,33},{49,65},{8... | collective-permute-start | bytes 786440 | tf_op jit(solution)/shard_map/ppermute | solution.py:237
  7.0 0.1 collective-permute-start
  7.1 0.7 pad_convert_fusion.taps_ref
  7.8 5.8 %filter_interior.1 = (bf16[16,2,4,64,256]{4,3,2,1,0:T(8,128)(2,1)}, bf16[4,2,256,256]{3,2,1,0:T(8,128)(2,1)S(1)}, bf16[2,2,4,192,256]{4,3,2,1,0:T(8,128)(2,1)S(1)}, f32[64,256]{1,0:T(8,128)S(1)}) custom-call(f32[2,4,256]{2,1,0:T(4,128)S(1)} %pad_convert_fusion.taps_ref, s32[2,256]{1,0:T(2,128)} %bitcast.2, bf16[2,4,1024,256]{3,2,1,0:T(8,128)(2,1)} %image_ref.1), custom_call_target="tpu_custom_call" | custom-call | flops 2000000000 | bytes 9000000 | tf_op jit(solution)/shard_map/filter_interior/pallas_call | solution.py:258
  13.6 1.0 %collective-permute-done.1.odd_pairs_ref = bf16[2,4,64,256]{3,2,1,0:T(8,128)(2,1)S(1)} collective-permute-done((bf16[2,4,64,256]{3,2,1,0:T(8,128)(2,1)S(1)}, bf16[2,4,64,256]{3,2,1,0:T(8,128)(2,1)S(1)}, u32[]{:S(2)}, u32[]{:S(2)}) %collective-permute-start.1) | collective-permute-done | bytes 262176 | tf_op jit(solution)/shard_map/ppermute | solution.py:237
  14.6 0.2 collective-permute-done.even_ref
  14.8 1.7 %filter_edges.1 = bf16[16,2,4,64,256]{4,3,2,1,0:T(8,128)(2,1)} custom-call(s32[1]{0:T(128)} %bitcast.1.odd_ref, bf16[4,2,256,256]{3,2,1,0:T(8,128)(2,1)S(1)} %get-tuple-element.10.band_ref, bf16[2,2,4,192,256]{4,3,2,1,0:T(8,128)(2,1)S(1)} %get-tuple-element.11.edge_ref, ...), custom_call_target="tpu_custom_call", output_to_operand_aliasing={{}: (5, {})} | custom-call | flops 2000000000 | bytes 9000000 | tf_op jit(solution)/shard_map/filter_edges/pallas_call | solution.py:279
  16.6 0.0 copy-start
  16.6 56.3 %all_to_all.5.got = bf16[16,2,4,64,256]{4,3,2,1,0:T(8,128)(2,1)S(1)} all-to-all(bf16[16,2,4,64,256]{4,3,2,1,0:T(8,128)(2,1)} %filter_edges.1), channel_id=1, replica_groups=mesh['az'=8,'acq'=16] {'acq'}, dimensions={0} | all-to-all | bytes 8388608 | tf_op jit(solution)/shard_map/all_to_all | solution.py:292
  72.9 0.0 copy-done
  72.9 6.6 %pairs_and_inversion.1 = f32[64,1024]{1,0:T(8,128)} custom-call(s32[2,256]{1,0:T(2,128)S(1)} %bitcast.3, f32[64,256]{1,0:T(8,128)S(1)} %get-tuple-element.9.map_ref, bf16[16,2,4,64,256]{4,3,2,1,0:T(8,128)(2,1)S(1)} %all_to_all.5.got), custom_call_target="tpu_custom_call" | custom-call | flops 2000000000 | bytes 9000000 | tf_op jit(solution)/shard_map/pairs_and_inversion/pallas_call | solution.py:293
Async XLA Ops:
  1.1 13.6 %collective-permute-start.1 = (bf16[2,4,64,256]{3,2,1,0:T(8,128)(2,1)S(1)}, bf16[2,4,64,256]{3,2,1,0:T(8,128)(2,1)S(1)}, u32[]{:S(2)}, u32[]{:S(2)}) collective-permute-start(bf16[2,4,64,256]{3,2,1,0:T(8,128)(2,1)S(1)} %get-tuple-element.13), channel_id=1, source_target_pairs={{16,32},{48,64},{80,96},{32,16},{64,48},{96,80},{17,33},{49,65},{8... | collective-permute-start | bytes 786440 | tf_op jit(solution)/shard_map/ppermute | solution.py:237
  7.0 7.8 %collective-permute-start = (bf16[2,4,64,256]{3,2,1,0:T(8,128)(2,1)S(1)}, bf16[2,4,64,256]{3,2,1,0:T(8,128)(2,1)S(1)}, u32[]{:S(2)}, u32[]{:S(2)}) collective-permute-start(bf16[2,4,64,256]{3,2,1,0:T(8,128)(2,1)S(1)} %get-tuple-element.14), channel_id=1, source_target_pairs={{0,16},{32,48},{64,80},{96,112},{16,0},{48,32},{80,64},{112,96},{1... | collective-permute-start | bytes 786440 | tf_op jit(solution)/shard_map/ppermute | solution.py:237
  16.6 56.3 %copy-start = (s32[256,2]{0,1:T(2,128)S(1)}, s32[256,2]{0,1:T(2,128)}, u32[]{:S(2)}) copy-start(s32[256,2]{0,1:T(2,128)} %param.5) | copy-start | bytes 6148

commit v6 on v5

--- a/solution.py
+++ b/solution.py
@@ -138,7 +138,18 @@
         copy.wait()
 
 
-def edge_kernel(odd_ref, band_ref, edge_ref, even_ref, odd_pairs_ref, filled_ref, out_ref, done, left):
+def halo_kernel(odd_ref, image_ref, even_ref, odd_pairs_ref, arrived):
+    rows = image_ref.shape[2]
+    copies = []
+    for start, out_ref in enumerate((even_ref, odd_pairs_ref)):
+        at = pl.multiple_of(jnp.where(odd_ref[0] == start, rows - HALO, 0), HALO)
+        copies.append(pltpu.make_async_copy(image_ref.at[:, :, pl.ds(at, HALO)], out_ref, arrived.at[start]))
+        copies[-1].start()
+    for copy in copies:
+        copy.wait()
+
+
+def edge_kernel(odd_ref, band_ref, edge_ref, odd_pairs_ref, even_ref, filled_ref, out_ref, done, left):
     del filled_ref
     local, columns = even_ref.shape[1], even_ref.shape[3]
     order = column_order(columns)
@@ -233,13 +244,17 @@
     total_acq = groups * local
     odd = lax.axis_index("az") % 2
     meet = [[(i, i + 1) for i in range(start, blocks_az - 1, 2)] for start in range(2)]
-    even_pairs, odd_pairs = (
-        lax.ppermute(
-            lax.dynamic_slice_in_dim(radar_stack, jnp.where(odd == start, rows - HALO, 0), HALO, 2),
-            "az",
-            ones + [(j, i) for i, j in ones],
-        )
-        for start, ones in enumerate(meet)
+    halo = pltpu.VMEM((2, local, HALO, columns), radar_stack.dtype)
+    sent = pl.pallas_call(
+        halo_kernel,
+        in_specs=[SMEM, HBM],
+        out_specs=[VMEM] * 2,
+        out_shape=[halo] * 2,
+        scratch_shapes=[pltpu.SemaphoreType.DMA((2,))],
+        name="halo_rows",
+    )(odd.reshape(1), pltpu.with_memory_space_constraint(radar_stack, pltpu.HBM))
+    odd_pairs, even_pairs = (
+        lax.ppermute(sent[start], "az", meet[start] + [(j, i) for i, j in meet[start]]) for start in (1, 0)
     )
     taps = jnp.pad(band_taps.astype(jnp.float32), ((0, 0), (0, 0), (0, 2 * BLOCK - band_taps.shape[2])))
     pairs = pair_list.T
@@ -288,7 +303,7 @@
         ],
         name="filter_edges",
         **settings(24),
-    )(odd.reshape(1), band, edge, even_pairs, odd_pairs, filtered)
+    )(odd.reshape(1), band, edge, odd_pairs, even_pairs, filtered)
     got = lax.all_to_all(filtered, "acq", 0, 0, tiled=True)
     return pl.pallas_call(
         pair_kernel,

time: 79.7 us -> 79.7 us (level)
  local copies, waits for them, and re-layouts: 1.08 us -> 0.01 us
  Pallas kernels: 14.2 us -> 15.2 us
    dynamic_slice x1 -> x0, local copies, waits for them, and re-layouts: 1.07 us -> none  [per_device(): lax.dynamic_slice_in_dim(radar_stack, jnp.where(odd == start, rows - HALO...]
    pallas_call x0 -> x1, Pallas kernels: none -> 1.06 us  [per_device(): pl.pallas_call(halo_kernel, in_specs=[SMEM, HBM], out_specs=[VMEM] * 2, o...]
  transfers between devices with their start and end apart: 2 -> 2, of which waited for: 2 -> 2; matrix products, arithmetic and copies ran while one was open for 1% -> 0% of each run, Pallas kernels for 7% -> 7%
where the time goes in v6:
time: 79.7 us; the launch traced here: 79.5 us
  blocking collectives  56.3 us (71%)
  Pallas kernels  15.2 us (19%)
  starting transfers between devices  5.97 us (7%)
  waiting for transfers between devices  1.88 us (2%)
    all_to_all x1, blocking collectives, per_device(): got = lax.all_to_all(filtered, 'acq', 0, 0, tiled=True)  56.3 us
    pallas_call x1, Pallas kernels, per_device(): pl.pallas_call(pair_kernel, in_specs=[SMEM, VMEM, VMEM], out_specs=VMEM,...  6.58 us
    ppermute x2, starting transfers between devices, per_device(): lax.ppermute(sent[start], 'az', meet[start] + [(j, i) for i, j in meet[st...  5.97 us
    pallas_call x1, Pallas kernels, per_device(): pl.pallas_call(interior_kernel, in_specs=[VMEM, HBM, HBM], out_specs=[HBM...  5.84 us
    ppermute x2, waiting for transfers between devices, per_device(): lax.ppermute(sent[start], 'az', meet[start] + [(j, i) for i, j in meet[st...  1.88 us
    pallas_call x1, Pallas kernels, per_device(): pl.pallas_call(edge_kernel, in_specs=[SMEM] + [VMEM] * 4 + [HBM], out_spe...  1.74 us
  transfers between devices with their start and end apart: 2, of which 2 were waited for; matrix products, arithmetic and copies ran while one was open for 0% of the time, Pallas kernels for 7%

profile of v6, /device:TPU:4, one launch (start us, length us, event | category | flops | bytes accessed | tf_op | source)
XLA Modules:
  0.0 79.5 jit_solution(17143901536607910135)
XLA Ops:
  0.0 0.0 copy-start.1
  0.0 1.1 %halo_rows.1 = (bf16[2,4,64,256]{3,2,1,0:T(8,128)(2,1)S(1)}, bf16[2,4,64,256]{3,2,1,0:T(8,128)(2,1)S(1)}) custom-call(s32[1]{0:T(128)} %bitcast.1.odd_ref, bf16[2,4,1024,256]{3,2,1,0:T(8,128)(2,1)} %image_ref.3), custom_call_target="tpu_custom_call" | custom-call | tf_op jit(solution)/shard_map/halo_rows/pallas_call | solution.py:248
  1.1 5.9 %collective-permute-start = (bf16[2,4,64,256]{3,2,1,0:T(8,128)(2,1)S(1)}, bf16[2,4,64,256]{3,2,1,0:T(8,128)(2,1)S(1)}, u32[]{:S(2)}, u32[]{:S(2)}) collective-permute-start(bf16[2,4,64,256]{3,2,1,0:T(8,128)(2,1)S(1)} %get-tuple-element.14), channel_id=1, source_target_pairs={{16,32},{48,64},{80,96},{32,16},{64,48},{96,80},{17,33},{49,65},{8... | collective-permute-start | bytes 786440 | tf_op jit(solution)/shard_map/ppermute | solution.py:257
  7.0 0.1 collective-permute-start.1
  7.1 0.0 copy-done.1
  7.1 5.8 %filter_interior.1 = (bf16[16,2,4,64,256]{4,3,2,1,0:T(8,128)(2,1)}, bf16[4,2,256,256]{3,2,1,0:T(8,128)(2,1)S(1)}, bf16[2,2,4,192,256]{4,3,2,1,0:T(8,128)(2,1)S(1)}, f32[64,256]{1,0:T(8,128)S(1)}) custom-call(f32[2,4,256]{2,1,0:T(4,128)S(1)} %pad_convert_fusion.taps_ref, s32[2,256]{1,0:T(2,128)} %bitcast.2, bf16[2,4,1024,256]{3,2,1,0:T(8,128)(2,1)} %image_ref.3), custom_call_target="tpu_custom_call" | custom-call | flops 2000000000 | bytes 9000000 | tf_op jit(solution)/shard_map/filter_interior/pallas_call | solution.py:273
  12.9 1.7 %collective-permute-done.odd_pairs_ref = bf16[2,4,64,256]{3,2,1,0:T(8,128)(2,1)S(1)} collective-permute-done((bf16[2,4,64,256]{3,2,1,0:T(8,128)(2,1)S(1)}, bf16[2,4,64,256]{3,2,1,0:T(8,128)(2,1)S(1)}, u32[]{:S(2)}, u32[]{:S(2)}) %collective-permute-start) | collective-permute-done | bytes 262176 | tf_op jit(solution)/shard_map/ppermute | solution.py:257
  14.6 0.2 collective-permute-done.1.even_ref
  14.8 1.7 %filter_edges.1 = bf16[16,2,4,64,256]{4,3,2,1,0:T(8,128)(2,1)} custom-call(s32[1]{0:T(128)} %bitcast.1.odd_ref, bf16[4,2,256,256]{3,2,1,0:T(8,128)(2,1)S(1)} %get-tuple-element.12.band_ref, bf16[2,2,4,192,256]{4,3,2,1,0:T(8,128)(2,1)S(1)} %get-tuple-element.13.edge_ref, ...), custom_call_target="tpu_custom_call", output_to_operand_aliasing={{}: (5, {})} | custom-call | flops 2000000000 | bytes 9000000 | tf_op jit(solution)/shard_map/filter_edges/pallas_call | solution.py:294
  16.6 0.0 copy-start
  16.6 56.3 %all_to_all.5.got = bf16[16,2,4,64,256]{4,3,2,1,0:T(8,128)(2,1)S(1)} all-to-all(bf16[16,2,4,64,256]{4,3,2,1,0:T(8,128)(2,1)} %filter_edges.1), channel_id=1, replica_groups=mesh['az'=8,'acq'=16] {'acq'}, dimensions={0} | all-to-all | bytes 8388608 | tf_op jit(solution)/shard_map/all_to_all | solution.py:307
  72.9 0.0 copy-done
  72.9 6.6 %pairs_and_inversion.1 = f32[64,1024]{1,0:T(8,128)} custom-call(s32[2,256]{1,0:T(2,128)S(1)} %bitcast.3, f32[64,256]{1,0:T(8,128)S(1)} %get-tuple-element.11.map_ref, bf16[16,2,4,64,256]{4,3,2,1,0:T(8,128)(2,1)S(1)} %all_to_all.5.got), custom_call_target="tpu_custom_call" | custom-call | flops 2000000000 | bytes 9000000 | tf_op jit(solution)/shard_map/pairs_and_inversion/pallas_call | solution.py:308
  (1 shorter events, 0.0 us)
Async XLA Ops:
  0.0 7.1 %copy-start.1 = (bf16[2,4,127]{2,1,0:T(4,128)(2,1)S(1)}, bf16[2,4,127]{2,1,0:T(4,128)(2,1)}, u32[]{:S(2)}) copy-start(bf16[2,4,127]{2,1,0:T(4,128)(2,1)} %param.4) | copy-start | bytes 6100
  1.1 13.6 %collective-permute-start = (bf16[2,4,64,256]{3,2,1,0:T(8,128)(2,1)S(1)}, bf16[2,4,64,256]{3,2,1,0:T(8,128)(2,1)S(1)}, u32[]{:S(2)}, u32[]{:S(2)}) collective-permute-start(bf16[2,4,64,256]{3,2,1,0:T(8,128)(2,1)S(1)} %get-tuple-element.14), channel_id=1, source_target_pairs={{16,32},{48,64},{80,96},{32,16},{64,48},{96,80},{17,33},{49,65},{8... | collective-permute-start | bytes 786440 | tf_op jit(solution)/shard_map/ppermute | solution.py:257
  7.0 7.8 %collective-permute-start.1 = (bf16[2,4,64,256]{3,2,1,0:T(8,128)(2,1)S(1)}, bf16[2,4,64,256]{3,2,1,0:T(8,128)(2,1)S(1)}, u32[]{:S(2)}, u32[]{:S(2)}) collective-permute-start(bf16[2,4,64,256]{3,2,1,0:T(8,128)(2,1)S(1)} %get-tuple-element.15), channel_id=1, source_target_pairs={{0,16},{32,48},{64,80},{96,112},{16,0},{48,32},{80,64},{112,96},{1... | collective-permute-start | bytes 786440 | tf_op jit(solution)/shard_map/ppermute | solution.py:257
  16.6 56.3 %copy-start = (s32[256,2]{0,1:T(2,128)S(1)}, s32[256,2]{0,1:T(2,128)}, u32[]{:S(2)}) copy-start(s32[256,2]{0,1:T(2,128)} %param.5) | copy-start | bytes 6148

commit v7 on v5

--- a/solution.py
+++ b/solution.py
@@ -210,7 +210,7 @@
     for g in range(groups):
         for slot in range(slots):
             widen(g, slot)
-    lax.fori_loop(0, groups * slots, lambda i, carry: one_reference(i), None, unroll=16)
+    lax.fori_loop(0, groups * slots, lambda i, carry: one_reference(i), None, unroll=32)
 
     table = map_ref[...]
     acqs, pairs = table.shape

time: 79.7 us -> 79.6 us (level)
  no operation moved by 1% of the time
where the time goes in v7:
time: 79.6 us; the launch traced here: 79.4 us
  blocking collectives  56.3 us (71%)
  Pallas kernels  14.1 us (18%)
  starting transfers between devices  5.97 us (8%)
  waiting for transfers between devices  1.22 us (2%)
  local copies, waits for them, and re-layouts  1.08 us (1%)
    all_to_all x1, blocking collectives, per_device(): got = lax.all_to_all(filtered, 'acq', 0, 0, tiled=True)  56.3 us
    pallas_call x1, Pallas kernels, per_device(): pl.pallas_call(pair_kernel, in_specs=[SMEM, VMEM, VMEM], out_specs=VMEM,...  6.47 us
    ppermute x2, starting transfers between devices, per_device(): lax.ppermute(lax.dynamic_slice_in_dim(radar_stack, jnp.where(odd == start...  5.97 us
    pallas_call x1, Pallas kernels, per_device(): pl.pallas_call(interior_kernel, in_specs=[VMEM, HBM, HBM], out_specs=[HBM...  5.84 us
    pallas_call x1, Pallas kernels, per_device(): pl.pallas_call(edge_kernel, in_specs=[SMEM] + [VMEM] * 4 + [HBM], out_spe...  1.75 us
  transfers between devices with their start and end apart: 2, of which 2 were waited for; matrix products, arithmetic and copies ran while one was open for 1% of the time, Pallas kernels for 7%

profile of v7, /device:TPU:4, one launch (start us, length us, event | category | flops | bytes accessed | tf_op | source)
XLA Modules:
  0.0 79.4 jit_solution(10027323918083593883)
XLA Ops:
  0.0 1.1 %constant_dynamic-slice_fusion = (bf16[2,4,64,256]{3,2,1,0:T(8,128)(2,1)S(1)}, bf16[2,4,64,256]{3,2,1,0:T(8,128)(2,1)S(1)}) fusion(bf16[2,4,1024,256]{3,2,1,0:T(8,128)(2,1)} %image_ref.1, s32[]{:T(128)S(6)} %select_n.18, s32[]{:T(128)S(6)} %select_n.17), kind=kLoop, calls=%fused_computation.1 | loop fusion | bytes 1048584 | tf_op jit(solution)/shard_map/dynamic_slice | solution.py:238
  1.1 5.9 %collective-permute-start.1 = (bf16[2,4,64,256]{3,2,1,0:T(8,128)(2,1)S(1)}, bf16[2,4,64,256]{3,2,1,0:T(8,128)(2,1)S(1)}, u32[]{:S(2)}, u32[]{:S(2)}) collective-permute-start(bf16[2,4,64,256]{3,2,1,0:T(8,128)(2,1)S(1)} %get-tuple-element.13), channel_id=1, source_target_pairs={{16,32},{48,64},{80,96},{32,16},{64,48},{96,80},{17,33},{49,65},{8... | collective-permute-start | bytes 786440 | tf_op jit(solution)/shard_map/ppermute | solution.py:237
  7.0 0.1 collective-permute-start
  7.1 0.7 pad_convert_fusion.taps_ref
  7.8 5.8 %filter_interior.1 = (bf16[16,2,4,64,256]{4,3,2,1,0:T(8,128)(2,1)}, bf16[4,2,256,256]{3,2,1,0:T(8,128)(2,1)S(1)}, bf16[2,2,4,192,256]{4,3,2,1,0:T(8,128)(2,1)S(1)}, f32[64,256]{1,0:T(8,128)S(1)}) custom-call(f32[2,4,256]{2,1,0:T(4,128)S(1)} %pad_convert_fusion.taps_ref, s32[2,256]{1,0:T(2,128)} %bitcast.2, bf16[2,4,1024,256]{3,2,1,0:T(8,128)(2,1)} %image_ref.1), custom_call_target="tpu_custom_call" | custom-call | flops 2000000000 | bytes 9000000 | tf_op jit(solution)/shard_map/filter_interior/pallas_call | solution.py:258
  13.6 1.0 %collective-permute-done.1.odd_pairs_ref = bf16[2,4,64,256]{3,2,1,0:T(8,128)(2,1)S(1)} collective-permute-done((bf16[2,4,64,256]{3,2,1,0:T(8,128)(2,1)S(1)}, bf16[2,4,64,256]{3,2,1,0:T(8,128)(2,1)S(1)}, u32[]{:S(2)}, u32[]{:S(2)}) %collective-permute-start.1) | collective-permute-done | bytes 262176 | tf_op jit(solution)/shard_map/ppermute | solution.py:237
  14.6 0.2 collective-permute-done.even_ref
  14.8 1.7 %filter_edges.1 = bf16[16,2,4,64,256]{4,3,2,1,0:T(8,128)(2,1)} custom-call(s32[1]{0:T(128)} %bitcast.1.odd_ref, bf16[4,2,256,256]{3,2,1,0:T(8,128)(2,1)S(1)} %get-tuple-element.10.band_ref, bf16[2,2,4,192,256]{4,3,2,1,0:T(8,128)(2,1)S(1)} %get-tuple-element.11.edge_ref, ...), custom_call_target="tpu_custom_call", output_to_operand_aliasing={{}: (5, {})} | custom-call | flops 2000000000 | bytes 9000000 | tf_op jit(solution)/shard_map/filter_edges/pallas_call | solution.py:279
  16.6 0.0 copy-start
  16.6 56.3 %all_to_all.5.got = bf16[16,2,4,64,256]{4,3,2,1,0:T(8,128)(2,1)S(1)} all-to-all(bf16[16,2,4,64,256]{4,3,2,1,0:T(8,128)(2,1)} %filter_edges.1), channel_id=1, replica_groups=mesh['az'=8,'acq'=16] {'acq'}, dimensions={0} | all-to-all | bytes 8388608 | tf_op jit(solution)/shard_map/all_to_all | solution.py:292
  72.9 0.0 copy-done
  72.9 6.5 %pairs_and_inversion.1 = f32[64,1024]{1,0:T(8,128)} custom-call(s32[2,256]{1,0:T(2,128)S(1)} %bitcast.3, f32[64,256]{1,0:T(8,128)S(1)} %get-tuple-element.9.map_ref, bf16[16,2,4,64,256]{4,3,2,1,0:T(8,128)(2,1)S(1)} %all_to_all.5.got), custom_call_target="tpu_custom_call" | custom-call | flops 2000000000 | bytes 9000000 | tf_op jit(solution)/shard_map/pairs_and_inversion/pallas_call | solution.py:293
Async XLA Ops:
  1.1 13.6 %collective-permute-start.1 = (bf16[2,4,64,256]{3,2,1,0:T(8,128)(2,1)S(1)}, bf16[2,4,64,256]{3,2,1,0:T(8,128)(2,1)S(1)}, u32[]{:S(2)}, u32[]{:S(2)}) collective-permute-start(bf16[2,4,64,256]{3,2,1,0:T(8,128)(2,1)S(1)} %get-tuple-element.13), channel_id=1, source_target_pairs={{16,32},{48,64},{80,96},{32,16},{64,48},{96,80},{17,33},{49,65},{8... | collective-permute-start | bytes 786440 | tf_op jit(solution)/shard_map/ppermute | solution.py:237
  7.0 7.8 %collective-permute-start = (bf16[2,4,64,256]{3,2,1,0:T(8,128)(2,1)S(1)}, bf16[2,4,64,256]{3,2,1,0:T(8,128)(2,1)S(1)}, u32[]{:S(2)}, u32[]{:S(2)}) collective-permute-start(bf16[2,4,64,256]{3,2,1,0:T(8,128)(2,1)S(1)} %get-tuple-element.14), channel_id=1, source_target_pairs={{0,16},{32,48},{64,80},{96,112},{16,0},{48,32},{80,64},{112,96},{1... | collective-permute-start | bytes 786440 | tf_op jit(solution)/shard_map/ppermute | solution.py:237
  16.6 56.3 %copy-start = (s32[256,2]{0,1:T(2,128)S(1)}, s32[256,2]{0,1:T(2,128)}, u32[]{:S(2)}) copy-start(s32[256,2]{0,1:T(2,128)} %param.5) | copy-start | bytes 6148
